TPU v7x, 32 devices: a whole 2x2x4 slice. The times are simulated.
32 devices in a mesh: rep: 8 (over z, core), shard: 4 (over y, x).
Axes of the slice: x: 2, y: 2, z: 4, core: 2. Of those that a mesh axis runs over, the one named last changes fastest.
Arguments:
- hidden_in: bfloat16 [32768, 1024], P(('rep', 'shard')), may hold values from -6 to 6
- cotangent: bfloat16 [32768, 1024], P(('rep', 'shard')), may hold values from -6 to 6
- lengths: int32 [32], P(('rep', 'shard')), may hold values from 64 to 1024, as said below
- weights: bfloat16 [1024, 12288], P('shard'), may hold values from -3 to 3
- moment_m: float32 [1024, 12288], P('shard'), may hold values from -60 to 60
- moment_v: float32 [1024, 12288], P('shard'), may hold values from 30 to 10000
- vectors: float32 [7168], replicated, may hold values from -2 to 2
- vector_m: float32 [7168], replicated, may hold values from -30 to 30
- vector_v: float32 [7168], replicated, may hold values from 10 to 10000
Outputs:
- hidden_out: bfloat16 [32768, 1024], P(('rep', 'shard'))
- grad_in: bfloat16 [32768, 1024], P(('rep', 'shard'))
- weight_grad: float32 [1024, 12288], P('shard')
- new_m: float32 [1024, 12288], P('shard')
- new_v: float32 [1024, 12288], P('shard')
- weight_update: float32 [1024, 12288], P('shard')
- vector_grad: float32 [7168], replicated
- vector_new_m: float32 [7168], replicated
- vector_new_v: float32 [7168], replicated
- vector_update: float32 [7168], replicated
Inputs may be any that keep to these rules, and one draw needn't show every extreme that they name: `lengths`: some sequence slot is full, of length 1024.
All inputs are finite; a program needn't handle non-finite values.
Results may differ from a plain program's by a relative error of at most 0.018.
Values may be sent and summed in bfloat16 or wider, within the bound.
No kernel may reach another device: no remote copies, remote signals or barrier semaphores. Data moves between devices by JAX's collectives and lax.ppermute only.
A program may use at most 512 MiB of HBM per device.

v0:
```python
import jax
import jax.numpy as jnp
from jax import lax
from jax.sharding import PartitionSpec as P

D = 1024
HEADS = 16
HEAD_DIM = 64
ROT = 32
FF = 4096
SEQ_LEN = 1024
STEP = 10


beta_one = 0.9
beta_two = 0.95
learn_rate = 0.02
decay_rate = 0.1
adam_eps = 1e-08
norm_epsilon = 1e-05
gelu_coef = 0.7978845608028654


def rotary_tables(seq_len):
    inv_freq = jnp.power(jnp.float32(10000.0), -jnp.arange(0, ROT, 2, dtype=jnp.float32) / ROT)
    angles = jnp.arange(seq_len, dtype=jnp.float32)[:, None] * inv_freq[None, :]
    return (jnp.cos(angles), jnp.sin(angles))


def rotate(tensor, cos_table, sin_table):
    half_rot = ROT // 2
    cos_part = cos_table[:, None, :]
    sin_part = sin_table[:, None, :]
    first_half = tensor[..., :half_rot]
    second_half = tensor[..., half_rot:ROT]
    return jnp.concatenate(
        [
            first_half * cos_part - second_half * sin_part,
            second_half * cos_part + first_half * sin_part,
            tensor[..., ROT:],
        ],
        -1,
    )


def unrotate(tensor, cos_table, sin_table):
    half_rot = ROT // 2
    cos_part = cos_table[:, None, :]
    sin_part = sin_table[:, None, :]
    first_half = tensor[..., :half_rot]
    second_half = tensor[..., half_rot:ROT]
    return jnp.concatenate(
        [
            first_half * cos_part + second_half * sin_part,
            second_half * cos_part - first_half * sin_part,
            tensor[..., ROT:],
        ],
        -1,
    )


def gelu_slope(preact):
    inner = gelu_coef * (preact + 0.044715 * preact * preact * preact)
    tanh_val = jnp.tanh(inner)
    return 0.5 * (1.0 + tanh_val) + 0.5 * preact * (1.0 - tanh_val * tanh_val) * gelu_coef * (
        1.0 + 3.0 * 0.044715 * preact * preact
    )


def block_scores(queries, keys_rot, query_start, length):
    scores = jnp.einsum(
        "qhd,khd->hqk", queries, keys_rot, preferred_element_type=jnp.float32
    ) * HEAD_DIM ** (-0.5)
    query_pos = query_start + jnp.arange(queries.shape[0])
    key_pos = jnp.arange(keys_rot.shape[0])
    allowed = (key_pos[None, :] <= query_pos[:, None]) & (key_pos[None, :] < length)
    return jnp.where(allowed[None], scores, -1e30)


def attend(queries, keys_rot, values, length):
    block_rows = min(512, SEQ_LEN)
    outputs = []
    log_sums = []
    for query_start in range(0, SEQ_LEN, block_rows):
        scores = block_scores(
            queries[query_start : query_start + block_rows], keys_rot, query_start, length
        )
        row_max = jnp.max(scores, -1, keepdims=True)
        exp_scores = jnp.exp(scores - row_max)
        row_total = jnp.sum(exp_scores, -1, keepdims=True)
        attn_prob = (exp_scores / row_total).astype(jnp.bfloat16)
        outputs.append(
            jnp.einsum("hqk,khd->qhd", attn_prob, values, preferred_element_type=jnp.float32)
        )
        log_sums.append(row_max + jnp.log(row_total))
    return (jnp.concatenate(outputs, 0), jnp.concatenate(log_sums, 1))


def attend_back(queries, keys_rot, values, grad_out, log_sums, length):
    block_rows = min(512, SEQ_LEN)
    scale_val = HEAD_DIM ** (-0.5)
    grad_queries = []
    grad_keys = jnp.zeros(keys_rot.shape, jnp.float32)
    grad_values = jnp.zeros(values.shape, jnp.float32)
    for query_start in range(0, SEQ_LEN, block_rows):
        query_blk = queries[query_start : query_start + block_rows]
        grad_blk = grad_out[query_start : query_start + block_rows]
        scores = block_scores(query_blk, keys_rot, query_start, length)
        attn_prob = jnp.exp(scores - log_sums[:, query_start : query_start + block_rows])
        grad_prob = jnp.einsum("qhd,khd->hqk", grad_blk, values, preferred_element_type=jnp.float32)
        row_delta = jnp.sum(attn_prob * grad_prob, -1, keepdims=True)
        grad_score = (attn_prob * (grad_prob - row_delta)).astype(jnp.bfloat16)
        grad_queries.append(
            jnp.einsum("hqk,khd->qhd", grad_score, keys_rot, preferred_element_type=jnp.float32)
            * scale_val
        )
        grad_keys = (
            grad_keys
            + jnp.einsum("hqk,qhd->khd", grad_score, query_blk, preferred_element_type=jnp.float32)
            * scale_val
        )
        grad_values = grad_values + jnp.einsum(
            "hqk,qhd->khd",
            attn_prob.astype(jnp.bfloat16),
            grad_blk,
            preferred_element_type=jnp.float32,
        )
    return (jnp.concatenate(grad_queries, 0), grad_keys, grad_values)


def weight_terms(pairs):
    pieces = []
    for left_side, right_side in pairs:
        pieces.append(
            lax.dot_general(
                left_side, right_side, (((0,), (0,)), ((), ())), preferred_element_type=jnp.float32
            )
        )
    return jnp.concatenate(pieces, 1)


def adamw(gradient, first_m, second_v, current, decay, step_count):
    corr_one = 1.0 - jnp.power(jnp.float32(beta_one), step_count)
    corr_two = 1.0 - jnp.power(jnp.float32(beta_two), step_count)
    new_first = beta_one * first_m + (1.0 - beta_one) * gradient
    new_second = beta_two * second_v + (1.0 - beta_two) * gradient * gradient
    change = -learn_rate * (
        new_first / corr_one / (jnp.sqrt(new_second / corr_two) + adam_eps) + decay * current
    )
    return (new_first, new_second, change)


def on_device(
    hidden_in, cotangent, lengths, weights, moment_m, moment_v, vectors, vector_m, vector_v
):
    seq_count = lengths.shape[0]
    tok_rows = hidden_in.shape[0]
    valid_rows = (
        (jnp.arange(SEQ_LEN)[None, :] < lengths[:, None])
        .reshape(tok_rows)
        .astype(jnp.float32)[:, None]
    )
    norm_scale_factor = vectors[:D]
    norm_offset = vectors[D : 2 * D]
    out_bias = vectors[2 * D : 3 * D]
    in_bias = vectors[3 * D :]
    contract_last = (((1,), (1,)), ((), ()))
    gathered = lax.all_gather(weights, "shard", axis=0, tiled=True)
    resid = hidden_in.astype(jnp.float32)
    row_mean = jnp.mean(resid, -1, keepdims=True)
    centered_rows = resid - row_mean
    row_variance = jnp.mean(centered_rows * centered_rows, -1, keepdims=True)
    inverse_deviation = lax.rsqrt(row_variance + norm_epsilon)
    standardized_input = centered_rows * inverse_deviation
    normalized_input = (standardized_input * norm_scale_factor + norm_offset).astype(jnp.bfloat16)
    projected = jnp.dot(normalized_input, gathered[:, : 3 * D], preferred_element_type=jnp.float32)
    preact = (
        jnp.dot(
            normalized_input, gathered[:, 4 * D : 4 * D + FF], preferred_element_type=jnp.float32
        )
        + in_bias
    )
    hidden = jax.nn.gelu(preact, approximate=True).astype(jnp.bfloat16)
    cos_table, sin_table = rotary_tables(SEQ_LEN)
    projected = projected.reshape(seq_count, SEQ_LEN, 3, HEADS, HEAD_DIM)
    queries = rotate(projected[:, :, 0], cos_table, sin_table).astype(jnp.bfloat16)
    keys_rot = rotate(projected[:, :, 1], cos_table, sin_table).astype(jnp.bfloat16)
    values = projected[:, :, 2].astype(jnp.bfloat16)
    seq_index = 0
    seq_out, seq_lse = attend(
        queries[seq_index], keys_rot[seq_index], values[seq_index], lengths[seq_index]
    )
    attn_list = [seq_out]
    lse_list = [seq_lse]
    attn_o = jnp.stack(attn_list, 0).reshape(tok_rows, D).astype(jnp.bfloat16)
    attn_out = jnp.dot(attn_o, gathered[:, 3 * D : 4 * D], preferred_element_type=jnp.float32)
    mlp_out = (
        lax.dot_general(
            hidden, gathered[:, 4 * D + FF :], contract_last, preferred_element_type=jnp.float32
        )
        + out_bias
    )
    hidden_out = (valid_rows * (resid + attn_out + mlp_out)).astype(jnp.bfloat16)
    backward_w = lax.all_gather(weights, "shard", axis=0, tiled=True)
    grad_out = cotangent.astype(jnp.float32) * valid_rows
    grad_low = grad_out.astype(jnp.bfloat16)
    grad_hidden = jnp.dot(grad_low, backward_w[:, 4 * D + FF :], preferred_element_type=jnp.float32)
    grad_pre = (grad_hidden * gelu_slope(preact)).astype(jnp.bfloat16)
    grad_attn = lax.dot_general(
        grad_low, backward_w[:, 3 * D : 4 * D], contract_last, preferred_element_type=jnp.float32
    )
    grad_attn = grad_attn.astype(jnp.bfloat16).reshape(seq_count, SEQ_LEN, HEADS, HEAD_DIM)
    seq_index = 0
    grad_q, grad_k, grad_v = attend_back(
        queries[seq_index],
        keys_rot[seq_index],
        values[seq_index],
        grad_attn[seq_index],
        lse_list[seq_index],
        lengths[seq_index],
    )
    grad_q = unrotate(grad_q, cos_table, sin_table)
    grad_k = unrotate(grad_k, cos_table, sin_table)
    grad_seqs = [jnp.stack([grad_q, grad_k, grad_v], 1)]
    grad_proj = jnp.stack(grad_seqs, 0).reshape(tok_rows, 3 * D).astype(jnp.bfloat16)
    normed_gradient = lax.dot_general(
        grad_proj, backward_w[:, : 3 * D], contract_last, preferred_element_type=jnp.float32
    )
    normed_gradient = normed_gradient + lax.dot_general(
        grad_pre,
        backward_w[:, 4 * D : 4 * D + FF],
        contract_last,
        preferred_element_type=jnp.float32,
    )
    standardized_gradient = normed_gradient * norm_scale_factor
    grad_ln = inverse_deviation * (
        standardized_gradient
        - jnp.mean(standardized_gradient, -1, keepdims=True)
        - standardized_input
        * jnp.mean(standardized_gradient * standardized_input, -1, keepdims=True)
    )
    grad_in = (grad_out + grad_ln).astype(jnp.bfloat16)
    vector_local = jnp.concatenate(
        [
            jnp.sum(normed_gradient * standardized_input, 0),
            jnp.sum(normed_gradient, 0),
            jnp.sum(grad_out, 0),
            jnp.sum(grad_pre.astype(jnp.float32), 0),
        ],
        0,
    )
    vector_grad = lax.psum(vector_local, ("rep", "shard"))
    pairs = [
        (normalized_input, grad_proj),
        (attn_o, grad_low),
        (normalized_input, grad_pre),
        (grad_low, hidden),
    ]
    group_rows = lax.psum_scatter(
        weight_terms(pairs).astype(jnp.bfloat16), "shard", scatter_dimension=0, tiled=True
    )
    weight_grad = lax.psum(group_rows, "rep").astype(jnp.float32)
    step_count = jnp.float32(STEP)
    new_m, new_v, weight_update = adamw(
        weight_grad, moment_m, moment_v, weights.astype(jnp.float32), decay_rate, step_count
    )
    vec_m, vec_v, vec_update = adamw(vector_grad, vector_m, vector_v, vectors, 0.0, step_count)
    return (
        hidden_out,
        grad_in,
        weight_grad,
        new_m,
        new_v,
        weight_update,
        vector_grad,
        vec_m,
        vec_v,
        vec_update,
    )


def solution(mesh):
    placed = (
        P(("rep", "shard"), None),
        P(("rep", "shard"), None),
        P(("rep", "shard")),
        P("shard", None),
        P("shard", None),
        P("shard", None),
        P(),
        P(),
        P(),
    )
    return jax.shard_map(
        on_device,
        mesh=mesh,
        in_specs=placed,
        out_specs=(
            P(("rep", "shard"), None),
            P(("rep", "shard"), None),
            P("shard", None),
            P("shard", None),
            P("shard", None),
            P("shard", None),
            P(),
            P(),
            P(),
            P(),
        ),
        check_vma=False,
    )
```

profile of v0, /device:TPU:0, one launch (start us, length us, event | category | flops | bytes accessed | tf_op | source)
XLA Modules:
  0.0 1053.4 jit_solution(8726561443215442701)
XLA Ops:
  13.4 227.0 %all-gather.2.cloned.1.call-done = bf16[1024,12288]{1,0:T(8,128)(2,1)} async-done(((bf16[256,12288]{1,0:T(8,128)(2,1)}), bf16[1024,12288]{1,0:T(8,128)(2,1)}) %all-gather.2.cloned.1.call-update) | async-done | bytes 25165840 | tf_op jit(solution)/shard_map/all_gather | solution.py:168
  240.3 9.7 fusion.37
  259.7 13.8 %fusion.102 = (f32[16,512]{1,0:T(8,128)S(1)}, f32[16,512,1024]{2,1,0:T(8,128)}) fusion(bf16[1024,16,32]{0,2,1:T(8,128)(2,1)S(1)} %fusion.78, bf16[1024,16,16]{0,2,1:T(8,128)(2,1)S(1)} %copy-done.12, bf16[1024,16,16]{0,2,1:T(8,128)(2,1)S(1)} %get-tuple-element.27, bf16[1,1024,16,64]{1,3,2,0:T(8,128)(2,1)S(1)} %pad_maximum_fusion.3, ...), kind=kOutput, calls=%fused_computation.159 | convolution fusion | flops 1105190912 | bytes 37257216 | tf_op jit(solution)/shard_map/qhd,khd->hqk/dot_general | solution.py:71
  273.4 14.3 %fusion.1 = f32[16,512]{1,0:T(8,128)S(1)} fusion(f32[16,512,1024]{2,1,0:T(8,128)} %get-tuple-element.47, f32[16,512]{1,0:T(8,128)S(1)} %get-tuple-element.46), kind=kLoop, calls=%fused_computation.13 | loop fusion | flops 16769024 | bytes 33619968 | tf_op jit(solution)/shard_map/reduce_sum | solution.py:90
  287.8 15.6 %fusion.77 = bf16[512,16,64]{0,2,1:T(8,128)(2,1)} fusion(f32[16,512,1024]{2,1,0:T(8,128)} %get-tuple-element.47, f32[16,512]{1,0:T(8,128)S(1)} %fusion.1, f32[16,512]{1,0:T(8,128)S(1)} %get-tuple-element.46, f32[1,1024,3,16,64]{1,4,3,2,0:T(8,128)} %bitcast.69), kind=kOutput, calls=%fused_computation.122 | convolution fusion | flops 1099431936 | bytes 36765696 | tf_op jit(solution)/shard_map/hqk,khd->qhd/dot_general | solution.py:93
  308.6 15.4 %fusion.19 = f32[16,64,1024]{2,1,0:T(8,128)} fusion(bf16[512,16,64]{0,2,1:T(8,128)(2,1)S(1)} %bitcast.77, f32[16,512,1024]{2,1,0:T(8,128)} %get-tuple-element.47, f32[16,512]{1,0:T(8,128)S(1)} %log_add_fusion), kind=kOutput, calls=%fused_computation.36 | convolution fusion | flops 1090519040 | bytes 38830080 | tf_op jit(solution)/shard_map/hqk,qhd->khd/dot_general | solution.py:122
  323.9 24.5 %multiply_reduce_fusion = (f32[16,512]{1,0:T(8,128)}, f32[16,512,1024]{2,1,0:T(8,128)}) fusion(f32[16,512,1024]{2,1,0:T(8,128)} %get-tuple-element.47, f32[16,512]{1,0:T(8,128)S(1)} %log_add_fusion, bf16[512,16,64]{0,2,1:T(8,128)(2,1)S(1)} %bitcast.78, f32[1,1024,3,16,64]{1,4,3,2,0:T(8,128)} %bitcast.70), kind=kOutput, calls=%fused_computation.1 | convolution fusion | flops 1098899456 | bytes 70320128 | tf_op jit(solution)/shard_map/qhd,khd->hqk/dot_general | solution.py:110
  348.4 13.8 %fusion.103 = (f32[16,512]{1,0:T(8,128)S(1)}, f32[16,512,1024]{2,1,0:T(8,128)}) fusion(bf16[1024,16,32]{0,2,1:T(8,128)(2,1)S(1)} %fusion.78, bf16[1024,16,16]{0,2,1:T(8,128)(2,1)S(1)} %copy-done.12, bf16[1024,16,16]{0,2,1:T(8,128)(2,1)S(1)} %get-tuple-element.27, bf16[1,1024,16,64]{1,3,2,0:T(8,128)(2,1)S(1)} %pad_maximum_fusion.3, ...), kind=kOutput, calls=%fused_computation.160 | convolution fusion | flops 1105190912 | bytes 37257216 | tf_op jit(solution)/shard_map/qhd,khd->hqk/dot_general | solution.py:71
  362.2 14.3 %fusion = f32[16,512]{1,0:T(8,128)S(1)} fusion(f32[16,512,1024]{2,1,0:T(8,128)} %get-tuple-element.49, f32[16,512]{1,0:T(8,128)S(1)} %get-tuple-element.48), kind=kLoop, calls=%fused_computation.12 | loop fusion | flops 16769024 | bytes 33619968 | tf_op jit(solution)/shard_map/reduce_sum | solution.py:90
  376.6 16.2 %fusion.76 = bf16[512,16,64]{0,2,1:T(8,128)(2,1)} fusion(f32[16,512,1024]{2,1,0:T(8,128)} %get-tuple-element.49, f32[16,512]{1,0:T(8,128)S(1)} %fusion, f32[16,512]{1,0:T(8,128)S(1)} %get-tuple-element.48, f32[1,1024,3,16,64]{1,4,3,2,0:T(8,128)} %bitcast.71), kind=kOutput, calls=%fused_computation.121 | convolution fusion | flops 1099431936 | bytes 36765696 | tf_op jit(solution)/shard_map/hqk,khd->qhd/dot_general | solution.py:93
  392.8 24.4 %multiply_reduce_fusion.1 = (f32[16,512]{1,0:T(8,128)S(1)}, f32[16,512,1024]{2,1,0:T(8,128)}) fusion(f32[16,512,1024]{2,1,0:T(8,128)} %get-tuple-element.49, f32[16,512]{1,0:T(8,128)S(1)} %log_add_fusion.1, bf16[512,16,64]{0,2,1:T(8,128)(2,1)} %bitcast.75, f32[1,1024,3,16,64]{1,4,3,2,0:T(8,128)S(1)} %bitcast.74), kind=kOutput, calls=%fused_computation.4 | convolution fusion | flops 1098899456 | bytes 70320128 | tf_op jit(solution)/shard_map/qhd,khd->hqk/dot_general | solution.py:110
  417.2 27.8 %multiply_convert_fusion.1 = bf16[16,512,1024]{2,1,0:T(8,128)(2,1)} fusion(f32[16,512,1024]{2,1,0:T(8,128)} %get-tuple-element.51, f32[16,512,1024]{2,1,0:T(8,128)} %get-tuple-element.49, f32[16,512]{1,0:T(8,128)S(1)} %get-tuple-element.50, f32[16,512]{1,0:T(8,128)S(1)} %log_add_fusion.1), kind=kLoop, calls=%fused_computation.3 | loop fusion | flops 33554432 | bytes 83951616 | tf_op jit(solution)/shard_map/convert_element_type | solution.py:112
  445.0 11.3 %multiply_bitcast_fusion.2 = f32[512,16,64]{0,2,1:T(8,128)S(1)} fusion(bf16[16,512,1024]{2,1,0:T(8,128)(2,1)} %multiply_convert_fusion.1, bf16[1024,16,32]{0,2,1:T(8,128)(2,1)S(1)} %copy-done.8, bf16[1024,16,16]{0,2,1:T(8,128)(2,1)} %get-tuple-element.28, bf16[1024,16,16]{0,2,1:T(8,128)(2,1)} %copy-done.11), kind=kOutput, calls=%fused_computation.109 | convolution fusion | flops 1080557568 | bytes 20971520 | tf_op jit(solution)/shard_map/hqk,khd->qhd/dot_general | solution.py:114
  456.3 11.2 %fusion.81 = f32[16,64,1024]{2,1,0:T(8,128)} fusion(bf16[16,512,1024]{2,1,0:T(8,128)(2,1)} %multiply_convert_fusion.1, bf16[1,1024,16,64]{1,3,2,0:T(8,128)(2,1)} %copy-done.6), kind=kOutput, calls=%fused_computation.136 | convolution fusion | flops 1073741824 | bytes 22020096 | tf_op jit(solution)/shard_map/hqk,qhd->khd/dot_general | solution.py:119
  467.5 27.9 %multiply_convert_fusion = bf16[16,512,1024]{2,1,0:T(8,128)(2,1)} fusion(f32[16,512,1024]{2,1,0:T(8,128)} %get-tuple-element.53, f32[16,512,1024]{2,1,0:T(8,128)} %get-tuple-element.47, f32[16,512]{1,0:T(8,128)S(1)} %copy-done.30, f32[16,512]{1,0:T(8,128)S(1)} %copy-done.23), kind=kLoop, calls=%fused_computation | loop fusion | flops 33554432 | bytes 83951616 | tf_op jit(solution)/shard_map/convert_element_type | solution.py:112
  495.4 12.6 %multiply_bitcast_fusion.1 = f32[512,16,64]{0,2,1:T(8,128)} fusion(bf16[16,512,1024]{2,1,0:T(8,128)(2,1)} %multiply_convert_fusion, bf16[1024,16,32]{0,2,1:T(8,128)(2,1)S(1)} %copy-done.8, bf16[1024,16,16]{0,2,1:T(8,128)(2,1)} %get-tuple-element.28, bf16[1024,16,16]{0,2,1:T(8,128)(2,1)} %copy-done.11), kind=kOutput, calls=%fused_computation.108 | convolution fusion | flops 1080557568 | bytes 20971520 | tf_op jit(solution)/shard_map/hqk,khd->qhd/dot_general | solution.py:114
  508.0 10.4 multiply_bitcast_fusion
  523.7 15.1 %fusion.33 = f32[1024,4096]{1,0:T(8,128)} fusion(bf16[1024,12288]{1,0:T(8,128)(2,1)} %all-gather.2.cloned.1.call-done, bf16[1024,1024]{1,0:T(8,128)(2,1)S(1)} %copy-done.3, f32[1024]{0:T(1024)S(1)} %copy-done.47, f32[1024]{0:T(1024)S(1)} %copy-done.41, f32[1024]{0:T(1024)S(1)} %copy-done.43, f32[1024]{0:T(1024)S(1)} %copy-done.35), kind=kOutput, calls=%fused_computation.53 | convolution fusion | flops 8596226048 | bytes 27279360 | tf_op jit(solution)/shard_map/dot_general | solution.py:178
  538.8 15.6 %convolution_convert_fusion = bf16[1024,4096]{1,0:T(8,128)(2,1)} fusion(bf16[1024,1024]{1,0:T(8,128)(2,1)S(1)} %copy-done.17, f32[1024]{0:T(1024)S(1)} %copy-done.39, f32[1024,4096]{1,0:T(8,128)} %fusion.33, f32[4096]{0:T(1024)S(1)} %copy-done.44), kind=kOutput, calls=%fused_computation.46 | convolution fusion | flops 8639217664 | bytes 27283456 | tf_op jit(solution)/shard_map/dot_general | solution.py:135
  554.4 24.9 %convert_reduce_fusion = (f32[4096]{0:T(1024)S(1)}, bf16[1024,4096]{1,0:T(8,128)(2,1)}) fusion(f32[1024,4096]{1,0:T(8,128)} %fusion.33, f32[4096]{0:T(1024)S(1)} %copy-done.44, bf16[1024,12288]{1,0:T(8,128)(2,1)} %all-gather.2.cloned.1.call-done, bf16[1024,1024]{1,0:T(8,128)(2,1)} %param.10, f32[1024]{0:T(1024)S(1)} %copy-done.39), kind=kOutput, calls=%fused_computation.38 | convolution fusion | flops 8685350912 | bytes 35688448 | tf_op jit(solution)/shard_map/dot_general | solution.py:207
  579.3 15.5 %convolution_convert_fusion.1 = bf16[1024,4096]{1,0:T(8,128)(2,1)} fusion(bf16[1024,4096]{1,0:T(8,128)(2,1)} %get-tuple-element.56, bf16[1024,1024]{1,0:T(8,128)(2,1)S(1)} %copy-done.4, f32[1024]{0:T(1024)S(1)} %copy-done.47, f32[1024]{0:T(1024)S(1)} %copy-done.41, f32[1024]{0:T(1024)S(1)} %copy-done.43, f32[1024]{0:T(1024)S(1)} %copy-done.35), kind=kOutput, calls=%fused_computation.47 | convolution fusion | flops 8600420352 | bytes 18890752 | tf_op jit(solution)/shard_map/dot_general | solution.py:135
  594.8 16.2 %fusion.64 = bf16[1024,1,16,64]{0,3,2,1:T(8,128)(2,1)} fusion(f32[16,64,1024]{2,1,0:T(8,128)} %fusion.19, bf16[512,16,64]{0,2,1:T(8,128)(2,1)S(1)} %bitcast.76, f32[16,512,1024]{2,1,0:T(8,128)} %get-tuple-element.49, f32[16,512]{1,0:T(8,128)S(1)} %log_add_fusion.1), kind=kOutput, calls=%fused_computation.96 | convolution fusion | flops 1092616192 | bytes 40927232 | tf_op jit(solution)/shard_map/hqk,qhd->khd/dot_general | solution.py:122
  628.2 10.0 convolution_convert_fusion.2
  638.1 17.6 %pad_maximum_fusion = bf16[1024,12288]{1,0:T(8,128)(2,1)} fusion(bf16[1024,4096]{1,0:T(8,128)(2,1)} %convolution_convert_fusion, bf16[1024,4096]{1,0:T(8,128)(2,1)} %convolution_convert_fusion.1, bf16[1024,1024]{1,0:T(8,128)(2,1)} %copy.24, bf16[1024,3072]{1,0:T(8,128)(2,1)} %convolution_convert_fusion.2), kind=kLoop, calls=%fused_computation.16 | loop fusion | flops 100663296 | bytes 50331648 | tf_op jit(solution)/shard_map/concatenate | solution.py:139
  655.9 10.7 %fusion.35 = f32[1024,1024]{1,0:T(8,128)S(1)} fusion(bf16[1024,3072]{0,1:T(8,128)(2,1)} %bitcast.80, bf16[1024,12288]{1,0:T(8,128)(2,1)} %all-gather.2.cloned.1.call-done), kind=kOutput, calls=%fused_computation.60 | convolution fusion | flops 6442450944 | bytes 16777216 | tf_op jit(solution)/shard_map/dot_general | solution.py:226
  666.6 15.5 %fusion.52 = (f32[1024]{0:T(1024)S(1)}, f32[1024]{0:T(1024)S(1)}, f32[1024]{0:T(1024)S(1)}, f32[1024]{0:T(1024)S(1)}, f32[1024,1024]{1,0:T(8,128)S(1)}) fusion(bf16[1024,1024]{1,0:T(8,128)(2,1)S(1)} %copy-done.4, f32[1024]{0:T(1024)S(1)} %copy-done.43, f32[1024]{0:T(1024)S(1)} %copy-done.35, f32[1024]{0:T(1024)S(1)} %copy-done.41, ...), kind=kOutput, calls=%fused_computation.81 | convolution fusion | flops 8601464832 | bytes 27291648 | tf_op jit(solution)/shard_map/dot_general | solution.py:229
  685.3 40.3 %psum.15 = f32[7168]{0:T(1024)S(1)} all-reduce(f32[7168]{0:T(1024)S(1)} %pad_maximum_fusion.6), channel_id=1, replica_groups=mesh['rep'=8,'shard'=4] {'rep','shard'}, use_global_device_ids=true, to_apply=%region_16.17 | all-reduce | flops 7168 | bytes 57344 | tf_op jit(solution)/shard_map/psum | solution.py:252
  726.3 6.8 fusion.72
  733.2 146.1 %reduce-scatter.2.cloned.1.call-done = bf16[256,12288]{1,0:T(8,128)(2,1)} async-done(((bf16[1024,12288]{1,0:T(8,128)(2,1)}), bf16[256,12288]{1,0:T(8,128)(2,1)}) %reduce-scatter.2.cloned.1.call-update) | async-done | bytes 6291472 | tf_op jit(solution)/shard_map/reduce_scatter | solution.py:259
  879.3 18.6 %fusion.56 = bf16[1024,1024]{1,0:T(8,128)(2,1)} fusion(f32[1024,1024]{1,0:T(8,128)} %fusion.72, bf16[1024,1024]{1,0:T(8,128)(2,1)S(1)} %copy-done.4, bf16[1024,12288]{1,0:T(8,128)(2,1)} %all-gather.2.cloned.1.call-done, f32[1024]{0:T(1024)S(1)} %copy-done.45, f32[1024]{0:T(1024)S(1)} %copy-done.39, f32[1024,4096]{1,0:T(8,128)} %fusion.33, ...), kind=kOutput, calls=%fused_computation.85 | convolution fusion | flops 8638169088 | bytes 33579008 | tf_op jit(solution)/shard_map/dot_general | solution.py:198
  897.8 120.0 %all-reduce.2.cloned.1.call-done = bf16[256,12288]{1,0:T(8,128)(2,1)} async-done(((bf16[256,12288]{1,0:T(8,128)(2,1)}), bf16[256,12288]{1,0:T(8,128)(2,1)}) %all-reduce.2.cloned.1.call-update) | async-done | bytes 6291472 | tf_op jit(solution)/shard_map/psum | solution.py:262
  1017.8 28.7 %add_multiply_fusion = (f32[256,12288]{1,0:T(8,128)}, f32[256,12288]{1,0:T(8,128)}, f32[256,12288]{1,0:T(8,128)}, f32[256,12288]{1,0:T(8,128)}) fusion(bf16[256,12288]{1,0:T(8,128)(2,1)} %param.12, f32[256,12288]{1,0:T(8,128)} %param.14, f32[256,12288]{1,0:T(8,128)} %param.13, bf16[256,12288]{1,0:T(8,128)(2,1)} %all-reduce.2.cloned.1.call-done), kind=kLoop, calls=%fused_computation.44 | loop fusion | flops 50331648 | bytes 88080384 | tf_op jit(solution)/shard_map/mul | solution.py:147
  (143 shorter events, 46.5 us)
Async XLA Ops:
  7.2 233.1 %all-gather.2.cloned.1.call-start = ((), (), s32[]{:S(2)}) async-start(), calls=%async_computation.1 | async-start | bytes 31457280 | tf_op jit(solution)/shard_map/all_gather | solution.py:168
  7.9 871.3 %reduce-scatter.2.cloned.1.call-start = ((), (), s32[]{:S(2)}) async-start(), calls=%async_computation.2 | async-start | bytes 31457280 | tf_op jit(solution)/shard_map/reduce_scatter | solution.py:259
  9.3 294.1 %copy-start.38 = (f32[1024]{0:T(1024)}, f32[1024]{0:T(1024)S(1)}, u32[]{:S(2)}) copy-start(f32[1024]{0:T(1024)S(1)} %fusion.87) | copy-start | bytes 12292
  9.7 240.4 %copy-start.34 = (f32[1024]{0:T(1024)}, f32[1024]{0:T(1024)S(1)}, u32[]{:S(2)}) copy-start(f32[1024]{0:T(1024)S(1)} %broadcast_multiply_fusion.2) | copy-start | bytes 12292
  10.9 239.1 %copy-start.40 = (f32[1024]{0:T(1024)}, f32[1024]{0:T(1024)S(1)}, u32[]{:S(2)}) copy-start(f32[1024]{0:T(1024)S(1)} %get-tuple-element.41) | copy-start | bytes 12292
  10.9 239.2 %copy-start.42 = (f32[1024]{0:T(1024)}, f32[1024]{0:T(1024)S(1)}, u32[]{:S(2)}) copy-start(f32[1024]{0:T(1024)S(1)} %get-tuple-element.57) | copy-start | bytes 12292
  11.0 239.2 %copy-start.46 = (f32[1024]{0:T(1024)}, f32[1024]{0:T(1024)S(1)}, u32[]{:S(2)}) copy-start(f32[1024]{0:T(1024)S(1)} %get-tuple-element.40) | copy-start | bytes 12292
  255.5 92.9 %copy-start.7 = (bf16[1024,16,32]{0,2,1:T(8,128)(2,1)}, bf16[1024,16,32]{0,2,1:T(8,128)(2,1)S(1)}, u32[]{:S(2)}) copy-start(bf16[1024,16,32]{0,2,1:T(8,128)(2,1)S(1)} %fusion.78) | copy-start | bytes 3145732
  257.7 90.7 %copy-start.11 = (bf16[1024,16,16]{0,2,1:T(8,128)(2,1)}, bf16[1024,16,16]{0,2,1:T(8,128)(2,1)S(1)}, u32[]{:S(2)}) copy-start(bf16[1024,16,16]{0,2,1:T(8,128)(2,1)S(1)} %get-tuple-element.27) | copy-start | bytes 1572868
  258.0 90.5 %copy-start.6 = (bf16[1,1024,16,64]{1,3,2,0:T(8,128)(2,1)}, bf16[1,1024,16,64]{1,3,2,0:T(8,128)(2,1)S(1)}, u32[]{:S(2)}) copy-start(bf16[1,1024,16,64]{1,3,2,0:T(8,128)(2,1)S(1)} %pad_maximum_fusion.3) | copy-start | bytes 6291460
  287.8 36.2 %copy-start.22 = (f32[16,512]{1,0:T(8,128)}, f32[16,512]{1,0:T(8,128)S(1)}, u32[]{:S(2)}) copy-start(f32[16,512]{1,0:T(8,128)S(1)} %log_add_fusion) | copy-start | bytes 98308
  287.8 15.6 %copy-start.16 = (bf16[1024,1024]{1,0:T(8,128)(2,1)S(1)}, bf16[1024,1024]{1,0:T(8,128)(2,1)}, u32[]{:S(2)}) copy-start(bf16[1024,1024]{1,0:T(8,128)(2,1)} %param.10) | copy-start | bytes 6291460
  323.9 24.5 %copy-start.28 = (pred[512,1024]{1,0:T(8,128)(4,1)S(1)}, pred[512,1024]{1,0:T(8,128)(4,1)}, u32[]{:S(2)}) copy-start(pred[512,1024]{1,0:T(8,128)(4,1)} %get-tuple-element.42) | copy-start | bytes 1572868
  376.5 16.2 %slice-start = ((s8[12582912]{0:T(1024)(128)(4,1)}), s8[4194304]{0:T(1024)(128)(4,1)S(1)}, s32[]{:S(2)}) async-start(s8[12582912]{0:T(1024)(128)(4,1)} %bitcast.72), calls=%async_computation.4 | async-start | bytes 8388608
  376.5 16.2 %slice-start.1 = ((s8[12582912]{0:T(1024)(128)(4,1)}), s8[4194304]{0:T(1024)(128)(4,1)S(1)}, s32[]{:S(2)}) async-start(s8[12582912]{0:T(1024)(128)(4,1)} %bitcast.72), calls=%async_computation.5 | async-start | bytes 8388608
  376.6 16.2 %slice-start.2 = ((s8[12582912]{0:T(1024)(128)(4,1)}), s8[4194304]{0:T(1024)(128)(4,1)S(1)}, s32[]{:S(2)}) async-start(s8[12582912]{0:T(1024)(128)(4,1)} %bitcast.72), calls=%async_computation.6 | async-start | bytes 8388608
  417.2 27.8 %copy-start.8 = (bf16[1024,16,32]{0,2,1:T(8,128)(2,1)S(1)}, bf16[1024,16,32]{0,2,1:T(8,128)(2,1)}, u32[]{:S(2)}) copy-start(bf16[1024,16,32]{0,2,1:T(8,128)(2,1)} %copy-done.7) | copy-start | bytes 3145732
  456.3 11.2 %copy-start.23 = (f32[16,512]{1,0:T(8,128)S(1)}, f32[16,512]{1,0:T(8,128)}, u32[]{:S(2)}) copy-start(f32[16,512]{1,0:T(8,128)} %copy-done.22) | copy-start | bytes 98308
  508.0 11.7 %copy-start.1 = (f32[512,16,64]{0,2,1:T(8,128)S(1)}, f32[512,16,64]{0,2,1:T(8,128)}, u32[]{:S(2)}) copy-start(f32[512,16,64]{0,2,1:T(8,128)} %multiply_bitcast_fusion.1) | copy-start | bytes 6291460
  508.0 11.7 %copy-start.25 = (f32[1024,16]{0,1:T(8,128)S(1)}, f32[1024,16]{0,1:T(8,128)}, u32[]{:S(2)}) copy-start(f32[1024,16]{0,1:T(8,128)} %get-tuple-element.44) | copy-start | bytes 196612
  508.0 11.7 %copy-start.27 = (f32[1024,16]{0,1:T(8,128)S(1)}, f32[1024,16]{0,1:T(8,128)}, u32[]{:S(2)}) copy-start(f32[1024,16]{0,1:T(8,128)} %get-tuple-element.45) | copy-start | bytes 196612
  523.7 15.2 %copy-start.17 = (bf16[1024,1024]{1,0:T(8,128)(2,1)S(1)}, bf16[1024,1024]{1,0:T(8,128)(2,1)}, u32[]{:S(2)}) copy-start(bf16[1024,1024]{1,0:T(8,128)(2,1)} %param.10) | copy-start | bytes 6291460
  523.7 15.2 %copy-start.39 = (f32[1024]{0:T(1024)S(1)}, f32[1024]{0:T(1024)}, u32[]{:S(2)}) copy-start(f32[1024]{0:T(1024)} %copy-done.38) | copy-start | bytes 12292
  523.7 15.2 %copy-start.44 = (f32[4096]{0:T(1024)S(1)}, f32[4096]{0:T(1024)}, u32[]{:S(2)}) copy-start(f32[4096]{0:T(1024)} %slice.122) | copy-start | bytes 49156
  554.4 24.9 %copy-start.4 = (bf16[1024,1024]{1,0:T(8,128)(2,1)S(1)}, bf16[1024,1024]{1,0:T(8,128)(2,1)}, u32[]{:S(2)}) copy-start(bf16[1024,1024]{1,0:T(8,128)(2,1)} %param.9) | copy-start | bytes 6291460
  579.3 15.5 %copy-start.5 = (bf16[512,1024]{0,1:T(8,128)(2,1)S(1)}, bf16[512,1024]{0,1:T(8,128)(2,1)}, u32[]{:S(2)}) copy-start(bf16[512,1024]{0,1:T(8,128)(2,1)} %get-tuple-element.33) | copy-start | bytes 3145732
  655.8 362.0 %all-reduce.2.cloned.1.call-start = ((), (), s32[]{:S(2)}) async-start(), calls=%async_computation.3 | async-start | bytes 12582912 | tf_op jit(solution)/shard_map/psum | solution.py:262
  666.6 15.5 %copy-start.19 = (bf16[1024,1024]{1,0:T(8,128)(2,1)S(1)}, bf16[1024,1024]{1,0:T(8,128)(2,1)}, u32[]{:S(2)}) copy-start(bf16[1024,1024]{1,0:T(8,128)(2,1)} %param.10) | copy-start | bytes 6291460
  682.1 43.5 %copy-start.33 = (f32[7168]{0:T(1024)S(1)}, f32[7168]{0:T(1024)}, u32[]{:S(2)}) copy-start(f32[7168]{0:T(1024)} %param.15) | copy-start | bytes 86020
  682.1 43.5 %copy-start.36 = (f32[7168]{0:T(1024)S(1)}, f32[7168]{0:T(1024)}, u32[]{:S(2)}) copy-start(f32[7168]{0:T(1024)} %param.17) | copy-start | bytes 86020
  682.1 43.5 %copy-start.37 = (f32[7168]{0:T(1024)S(1)}, f32[7168]{0:T(1024)}, u32[]{:S(2)}) copy-start(f32[7168]{0:T(1024)} %param.16) | copy-start | bytes 86020
  733.2 146.1 %copy-start.45 = (f32[1024]{0:T(1024)S(1)}, f32[1024]{0:T(1024)}, u32[]{:S(2)}) copy-start(f32[1024]{0:T(1024)} %get-tuple-element.39) | copy-start | bytes 12292
  (22 other events, 61.3 us)
Sparse Core Ops, SparseCore 0:
  9.9 230.3 all-gather.1
  655.9 223.2 reduce-scatter.1
  881.7 136.0 all-reduce.1
where the time goes:
time: 1060 us; the launch traced here: 1050 us
  waiting for transfers between devices  494 us (47%)
  matrix products  336 us (32%)
  other arithmetic  148 us (14%)
  blocking collectives  40.3 us (4%)
  local copies, waits for them, and re-layouts  20.5 us (2%)
  between operations  15.3 us (1%)
    all_gather x1, waiting for transfers between devices, on_device(): gathered = lax.all_gather(weights, 'shard', axis=0, tiled=True)  227 us
    reduce_scatter x1, waiting for transfers between devices, on_device(): lax.psum_scatter(weight_terms(pairs).astype(jnp.bfloat16), 'shard', scatt...  146 us
    psum x1, waiting for transfers between devices, on_device(): weight_grad = lax.psum(group_rows, 'rep').astype(jnp.float32)  120 us
    convert_element_type x2, other arithmetic, attend_back(): grad_score = (attn_prob * (grad_prob - row_delta)).astype(jnp.bfloat16)  55.7 us
    dot_general x2, matrix products, attend_back(): jnp.einsum('qhd,khd->hqk', grad_blk, values, preferred_element_type=jnp.f...  48.9 us
    dot_general x4, matrix products, weight_terms(): lax.dot_general(left_side, right_side, (((0,), (0,)), ((), ())), preferre...  44.9 us
    psum x1, blocking collectives, on_device(): vector_grad = lax.psum(vector_local, ('rep', 'shard'))  40.3 us
    dot_general x2, matrix products, attend(): jnp.einsum('hqk,khd->qhd', attn_prob, values, preferred_element_type=jnp....  31.8 us
  transfers between devices with their start and end apart: 3, of which 3 were waited for; matrix products, arithmetic and copies ran while one was open for 6% of the time, Pallas kernels for 0%

commit v1 on v0

v1 whole, which is shorter than its diff:
```python
import functools

import jax
import jax.numpy as jnp
import numpy as np
from jax import lax
from jax.experimental import pallas as pl
from jax.experimental.pallas import tpu as pltpu
from jax.sharding import PartitionSpec as P

D = 1024
HEADS = 16
HEAD_DIM = 64
ROT = 32
FF = 4096
T = 1024
STEP = 10

B1 = 0.9
B2 = 0.95
LR = 0.02
DECAY = 0.1
ADAM_EPS = 1e-08
NORM_EPS = 1e-05
GC = 0.7978845608028654
GA = 0.044715
LOG2E = 1.4426950408889634
LN2 = 0.6931471805599453

BF = jnp.bfloat16
F32 = jnp.float32
VLIM = 58 * 1024 * 1024
NN = (((1,), (0,)), ((), ()))
NT = (((1,), (1,)), ((), ()))
TN = (((0,), (0,)), ((), ()))
TT = (((0,), (1,)), ((), ()))
TILE = 512
SIZES = (1536, 1536, 1024)
MB = 1024
TB = 256


def mm(a, b, dims=NN):
    return lax.dot_general(a, b, dims, preferred_element_type=F32)


def params():
    return pltpu.CompilerParams(
        dimension_semantics=("arbitrary",), vmem_limit_bytes=VLIM
    )


def once(shape):
    return pl.BlockSpec(shape, lambda *_: (0,) * len(shape), pipeline_mode=pl.Buffered(1))


def cost(flops, nbytes, trans=0):
    return pl.CostEstimate(
        flops=int(flops), bytes_accessed=int(nbytes), transcendentals=int(trans)
    )


def prep_kernel(hr, blocks, ids, x_ref, c_ref, g_ref, b_ref, n_ref, nt_ref, d_ref, dt_ref, db_ref, s_ref):
    i = pl.program_id(0)
    x = x_ref[...].astype(F32)
    mean = jnp.mean(x, -1, keepdims=True)
    xc = x - mean
    var = jnp.mean(xc * xc, -1, keepdims=True)
    n = xc * lax.rsqrt(var + NORM_EPS) * g_ref[...] + b_ref[...]
    n_ref[...] = n.astype(BF)
    row = i * TB + lax.broadcasted_iota(jnp.int32, (TB, 1), 0)
    dy = jnp.where(row < ids[0], c_ref[...].astype(F32), 0.0)
    d_ref[...] = dy.astype(BF)

    @pl.when(i == 0)
    def _():
        db_ref[...] = jnp.zeros_like(db_ref)

    db_ref[...] += jnp.sum(dy, 0, keepdims=True)
    for val, out in ((n, nt_ref), (dy, dt_ref)):
        s_ref[...] = val.T.astype(BF)
        for b in range(2 * blocks):
            off = pl.multiple_of(ids[1 + b], hr)
            out[b * hr : (b + 1) * hr, :] = s_ref[pl.ds(off, hr), :]


def prep(ids, x, cot, gain, shift, hr, blocks):
    row = lambda i, *_: (i, 0)
    col = lambda i, *_: (0, i)
    fix = lambda i, *_: (0, 0)
    return pl.pallas_call(
        functools.partial(prep_kernel, hr, blocks),
        grid_spec=pltpu.PrefetchScalarGridSpec(
            num_scalar_prefetch=1,
            grid=(T // TB,),
            in_specs=[
                pl.BlockSpec((TB, D), row),
                pl.BlockSpec((TB, D), row),
                pl.BlockSpec((1, D), fix),
                pl.BlockSpec((1, D), fix),
            ],
            out_specs=[
                pl.BlockSpec((TB, D), row),
                pl.BlockSpec((D, TB), col),
                pl.BlockSpec((TB, D), row),
                pl.BlockSpec((D, TB), col),
                pl.BlockSpec((1, D), fix),
            ],
            scratch_shapes=[pltpu.VMEM((D, TB), BF)],
        ),
        out_shape=[
            jax.ShapeDtypeStruct((T, D), BF),
            jax.ShapeDtypeStruct((D, T), BF),
            jax.ShapeDtypeStruct((T, D), BF),
            jax.ShapeDtypeStruct((D, T), BF),
            jax.ShapeDtypeStruct((1, D), F32),
        ],
        compiler_params=params(),
        cost_estimate=cost(T * D * 20, T * D * 12),
    )(ids, x, cot, gain, shift)


def place(dst, srcs, ids, base):
    for k, src in enumerate(srcs):
        rows = src.shape[0]
        dst[pl.ds(pl.multiple_of(ids[base + k], rows), rows), :] = src[...]


def mlp_kernel(np_, first, ids, n_ref, nt_ref, d_ref, dt_ref, b_ref, *refs):
    win = refs[:np_]
    wout = refs[np_ : 2 * np_]
    refs = refs[2 * np_ :]
    if not first:
        oin, gin = refs[:2]
        refs = refs[2:]
    gm_ref, gt_ref, db_ref, o_ref, g_ref, wi, wo, h_s, p_s = refs
    j = pl.program_id(0)
    place(wi, win, ids, 0)
    place(wo, wout, ids, 0)
    bias = b_ref[...]
    wi_v = wi[...]
    wo_v = wo[...]
    db = jnp.zeros((1, TILE), F32)
    for t in range(T // MB):
        rows = slice(t * MB, (t + 1) * MB)
        pre = mm(n_ref[rows, :], wi_v) + bias
        dh = mm(d_ref[rows, :], wo_v)
        sq = pre * pre
        th = jnp.tanh(GC * pre * (1.0 + GA * sq))
        half = 0.5 * (1.0 + th)
        h = (pre * half).astype(BF)
        slope = half + 0.5 * pre * (1.0 - th * th) * (GC + (3.0 * GA * GC) * sq)
        dp = (dh * slope).astype(BF)
        h_s[rows, :] = h
        p_s[rows, :] = dp
        db = db + jnp.sum(dp.astype(F32), 0, keepdims=True)
        ov = mm(h, wo_v, NT)
        gv = mm(wi_v, dp, NT)

        if first:

            @pl.when(j == 0)
            def _():
                o_ref[rows, :] = ov
                g_ref[:, rows] = gv

        else:

            @pl.when(j == 0)
            def _():
                o_ref[rows, :] = oin[rows, :] + ov
                g_ref[:, rows] = gin[:, rows] + gv

        @pl.when(j > 0)
        def _():
            o_ref[rows, :] += ov
            g_ref[:, rows] += gv

    db_ref[...] = db
    hv = h_s[...]
    pv = p_s[...]
    half_d = D // 2
    gt_ref[1] = mm(dt_ref[half_d:, :], hv).astype(BF)
    gt_ref[0] = mm(nt_ref[half_d:, :], pv).astype(BF)
    gm_ref[1] = mm(dt_ref[:half_d, :], hv).astype(BF)
    gm_ref[0] = mm(nt_ref[:half_d, :], pv).astype(BF)


def mlp(ids, n, nt, dy, dyt, bias, weights, pieces, offset, size, acc):
    first = acc is None
    nt_cols = size // TILE
    tall = lambda cols: pl.BlockSpec((T, cols), lambda j, *_: (0, 0))
    own_rows = weights.shape[0]
    in_base = (4 * D + offset) // TILE
    out_base = (4 * D + FF + offset) // TILE
    wspecs = []
    for base_own, base in ((in_base, offset // TILE), (out_base, (FF + offset) // TILE)):
        if own_rows:
            wspecs.append(pl.BlockSpec((own_rows, TILE), lambda j, *_, b=base_own: (0, b + j)))
        for p in pieces:
            wspecs.append(pl.BlockSpec((p.shape[0], TILE), lambda j, *_, b=base: (0, b + j)))
    wargs = [weights, *pieces]
    bb = offset // TILE
    gspec = pl.BlockSpec((2, D // 2, TILE), lambda j, *_: (0, 0, j))
    gshape = jax.ShapeDtypeStruct((2, D // 2, size), BF)
    return pl.pallas_call(
        functools.partial(mlp_kernel, len(wargs), first),
        grid_spec=pltpu.PrefetchScalarGridSpec(
            num_scalar_prefetch=1,
            grid=(nt_cols,),
            in_specs=[
                once((T, D)),
                once((D, T)),
                once((T, D)),
                once((D, T)),
                pl.BlockSpec((1, TILE), lambda j, *_: (0, bb + j)),
                *wspecs,
                *([] if first else [once((T, D)), once((D, T))]),
            ],
            out_specs=[
                gspec,
                gspec,
                pl.BlockSpec((1, TILE), lambda j, *_: (0, j)),
                once((T, D)),
                once((D, T)),
            ],
            scratch_shapes=[
                pltpu.VMEM((D, TILE), BF),
                pltpu.VMEM((D, TILE), BF),
                pltpu.VMEM((T, TILE), BF),
                pltpu.VMEM((T, TILE), BF),
            ],
        ),
        out_shape=[
            gshape,
            gshape,
            jax.ShapeDtypeStruct((1, size), F32),
            jax.ShapeDtypeStruct((T, D), F32),
            jax.ShapeDtypeStruct((D, T), F32),
        ],
        compiler_params=params(),
        cost_estimate=cost(12 * T * D * size, 8 * D * size + 24 * T * D, T * size),
    )(ids, n, nt, dy, dyt, bias, *wargs, *wargs, *([] if first else acc))


def proj_kernel(np_, ids, n_ref, d_ref, cos_ref, sin_ref, *refs):
    wq = refs[:np_]
    wo = refs[np_ : 2 * np_]
    out_ref, dout_ref, w_s, wo_s = refs[2 * np_ :]
    j = pl.program_id(0)
    place(w_s, wq, ids, 0)
    r = mm(w_s[...], n_ref[...], TT)

    def rotated(scale):
        for h in range(TB // HEAD_DIM):
            b = h * HEAD_DIM
            u = r[b : b + 16, :]
            w = r[b + 16 : b + 32, :]
            cs = cos_ref[...]
            sn = sin_ref[...]
            turned = [u * cs - w * sn, w * cs + u * sn, r[b + 32 : b + 64, :]]
            out_ref[b : b + 64, :] = (jnp.concatenate(turned, 0) * scale).astype(BF)

    @pl.when(j < 4)
    def _():
        rotated(LOG2E * HEAD_DIM ** (-0.5))

    @pl.when((j >= 4) & (j < 8))
    def _():
        rotated(1.0)

    @pl.when(j >= 8)
    def _():
        out_ref[...] = r.astype(BF)

    @pl.when(j == 0)
    def _():
        place(wo_s, wo, ids, 0)
        for t in range(D // TB):
            rows = slice(t * TB, (t + 1) * TB)
            dout_ref[rows, :] = mm(wo_s[rows, :], d_ref[...], NT).astype(BF)


def proj(ids, n, dy, cos, sin, weights, pieces):
    wargs = [weights, *pieces]
    return pl.pallas_call(
        functools.partial(proj_kernel, len(wargs)),
        grid_spec=pltpu.PrefetchScalarGridSpec(
            num_scalar_prefetch=1,
            grid=(3 * D // TB,),
            in_specs=[
                once((T, D)),
                once((T, D)),
                once((16, T)),
                once((16, T)),
                *[pl.BlockSpec((w.shape[0], TB), lambda j, *_: (0, j)) for w in wargs],
                *[
                    pl.BlockSpec((w.shape[0], D), lambda j, *_: (0, 3), pipeline_mode=pl.Buffered(1))
                    for w in wargs
                ],
            ],
            out_specs=[
                pl.BlockSpec((TB, T), lambda j, *_: (j, 0)),
                once((D, T)),
            ],
            scratch_shapes=[pltpu.VMEM((D, TB), BF), pltpu.VMEM((D, D), BF)],
        ),
        out_shape=[
            jax.ShapeDtypeStruct((3 * D, T), BF),
            jax.ShapeDtypeStruct((D, T), BF),
        ],
        compiler_params=params(),
        cost_estimate=cost(8 * T * D * D, 20 * T * D),
    )(ids, n, dy, cos, sin, *wargs, *wargs)


QB = 512
HPS = 2


def attn_kernel(n_alias, len_ref, q_ref, k_ref, v_ref, do_ref, cos_ref, sin_ref, *refs):
    o_ref, dq_ref, dk_ref, dv_ref = refs[n_alias:]
    sub = lax.broadcasted_iota(jnp.int32, (HEAD_DIM, T), 0)
    lane = lax.broadcasted_iota(jnp.int32, (HEAD_DIM, T), 1)
    bias = jnp.where((sub == 0) & (lane >= len_ref[0]), -1e30, 0.0)
    ones = jnp.where(sub == 0, 1.0, 0.0).astype(BF)
    none = jnp.zeros((HEAD_DIM, T), F32)
    ki = lax.broadcasted_iota(jnp.int32, (QB, QB), 0)
    qi = lax.broadcasted_iota(jnp.int32, (QB, QB), 1)

    def unrot(val, cs, sn, out, base, cols):
        a = val[0:16, :]
        b = val[16:32, :]
        turned = [a * cs + b * sn, b * cs - a * sn, val[32:64, :]]
        out[base : base + 64, cols] = jnp.concatenate(turned, 0).astype(BF)

    for h in range(HPS):
        b = h * HEAD_DIM
        hs = slice(b, b + HEAD_DIM)
        q = q_ref[hs, :]
        k = k_ref[hs, :]
        v = v_ref[hs, :]
        qa = jnp.concatenate([q, ones], 0)
        ka = jnp.concatenate([k.astype(F32), bias], 0).T.astype(BF)
        vt = jnp.concatenate([v.astype(F32), none], 0).T.astype(BF)
        dk = [jnp.zeros((HEAD_DIM, QB), F32) for _ in range(T // QB)]
        dv = [jnp.zeros((HEAD_DIM, QB), F32) for _ in range(T // QB)]
        for i in range(T // QB):
            qs = slice(i * QB, (i + 1) * QB)
            kk = (i + 1) * QB
            st = mm(ka[:kk, :], qa[:, qs])
            diag = jnp.where(ki <= qi, st[kk - QB :, :], -1e30)
            st = diag if i == 0 else jnp.concatenate([st[: kk - QB, :], diag], 0)
            e = jnp.exp2(st - jnp.max(st, 0, keepdims=True))
            rl = 1.0 / jnp.sum(e, 0, keepdims=True)
            eb = e.astype(BF)
            ot = mm(v[:, :kk], eb) * rl
            o_ref[hs, qs] = ot.astype(BF)
            dn = (do_ref[hs, qs].astype(F32) * rl).astype(BF)
            delta = jnp.sum(dn.astype(F32) * ot, 0, keepdims=True)
            da = jnp.concatenate([dn, none[:, qs].astype(BF)], 0)
            ds = (e * (mm(vt[:kk, :], da) - delta)).astype(BF)
            dq = mm(k[:, :kk], ds) * (HEAD_DIM ** (-0.5))
            unrot(dq, cos_ref[:, qs], sin_ref[:, qs], dq_ref, b, qs)
            dvi = mm(dn, eb, NT)
            dki = mm(q[:, qs], ds, NT)
            for t in range(i + 1):
                ts = slice(t * QB, (t + 1) * QB)
                dv[t] = dv[t] + dvi[:, ts]
                dk[t] = dk[t] + dki[:, ts]
        for t in range(T // QB):
            ts = slice(t * QB, (t + 1) * QB)
            dv_ref[hs, ts] = dv[t].astype(BF)
            unrot(dk[t] * LN2, cos_ref[:, ts], sin_ref[:, ts], dk_ref, b, ts)


def attend(length, qkv, dot_, cos, sin, first, heads, before):
    rows = HPS * HEAD_DIM
    steps = HEADS // HPS
    at = first // HPS
    spec = lambda base: pl.BlockSpec((rows, T), lambda h, *_: (base + at + h, 0))
    shape = jax.ShapeDtypeStruct((D, T), BF)
    alias = [] if before is None else list(before)
    return pl.pallas_call(
        functools.partial(attn_kernel, len(alias)),
        grid_spec=pltpu.PrefetchScalarGridSpec(
            num_scalar_prefetch=1,
            grid=(heads // HPS,),
            in_specs=[
                spec(0),
                spec(steps),
                spec(2 * steps),
                spec(0),
                once((16, T)),
                once((16, T)),
            ]
            + [pl.BlockSpec(memory_space=pl.ANY)] * len(alias),
            out_specs=[spec(0)] * 4,
        ),
        out_shape=[shape] * 4,
        input_output_aliases={7 + i: i for i in range(len(alias))},
        compiler_params=params(),
        cost_estimate=cost(12 * T * T * D, 18 * T * D, T * T * HEADS // 2),
    )(length, qkv, qkv, qkv, dot_, cos, sin, *alias)


def agrad_kernel(hr, order, blocks, ids, nt_ref, dy_ref, o_ref, dq_ref, dk_ref, dv_ref, m_ref, t_ref, g_s):
    j = pl.program_id(0)
    half_d = D // 2
    for at, src in enumerate((dq_ref, dk_ref, dv_ref)):

        @pl.when((j >= 2 * at) & (j < 2 * at + 2))
        def _(src=src):
            val = src[...]
            for out, first in ((m_ref, 0), (t_ref, half_d)):
                g = mm(nt_ref[first : first + half_d, :], val, NT).astype(BF)
                for b in range(blocks):
                    k = order[b]
                    out[0, b * hr : (b + 1) * hr, :] = g[k * hr : (k + 1) * hr, :]

    @pl.when(j >= 6)
    def _():
        g_s[...] = mm(o_ref[...], dy_ref[...]).astype(BF)
        for b in range(blocks):
            m_ref[0, b * hr : (b + 1) * hr, :] = g_s[pl.ds(pl.multiple_of(ids[b], hr), hr), :]
            t_ref[0, b * hr : (b + 1) * hr, :] = g_s[pl.ds(pl.multiple_of(ids[blocks + b], hr), hr), :]


def attn_grads(ids, nt, dy, ot, dq, dk, dv, hr, order):
    blocks = len(order)

    def grab(at):
        return pl.BlockSpec((TILE, T), lambda j, *_: (jnp.clip(j - 2 * at, 0, 1), 0))

    gspec = pl.BlockSpec((1, D // 2, TILE), lambda j, *_: (j // 4, 0, j % 4))
    gshape = jax.ShapeDtypeStruct((2, D // 2, 2 * D), BF)
    return pl.pallas_call(
        functools.partial(agrad_kernel, hr, order, blocks),
        grid_spec=pltpu.PrefetchScalarGridSpec(
            num_scalar_prefetch=1,
            grid=(4 * D // TILE,),
            in_specs=[
                once((D, T)),
                pl.BlockSpec((T, TILE), lambda j, *_: (0, jnp.clip(j - 6, 0, 1))),
                once((D, T)),
                grab(0),
                grab(1),
                grab(2),
            ],
            out_specs=[gspec, gspec],
            scratch_shapes=[pltpu.VMEM((D, TILE), BF)],
        ),
        out_shape=[gshape] * 2,
        compiler_params=params(),
        cost_estimate=cost(8 * T * D * D, 20 * T * D),
    )(ids, nt, dy, ot, dq, dk, dv)


def final_kernel(np_, ids, x_ref, dy_ref, g_ref, bo_ref, o_ref, dq_ref, dk_ref, dv_ref, ao_ref, ag_ref, *refs):
    wq = refs[:np_]
    out_ref, gin_ref, v_ref, w_s = refs[np_:]
    i = pl.program_id(0)

    @pl.when(i == 0)
    def _():
        place(w_s, wq, ids, 1)

    x = x_ref[...].astype(F32)
    row = i * TB + lax.broadcasted_iota(jnp.int32, (TB, 1), 0)
    attn = mm(o_ref[...], w_s[:, 3 * D :], TN)
    out = x + attn + ao_ref[...] + bo_ref[...]
    out_ref[...] = jnp.where(row < ids[0], out, 0.0).astype(BF)
    dn = (
        ag_ref[...]
        + mm(w_s[:, :D], dq_ref[...])
        + mm(w_s[:, D : 2 * D], dk_ref[...])
        + mm(w_s[:, 2 * D : 3 * D], dv_ref[...])
    ).T
    mean = jnp.mean(x, -1, keepdims=True)
    xc = x - mean
    inv = lax.rsqrt(jnp.mean(xc * xc, -1, keepdims=True) + NORM_EPS)
    xh = xc * inv
    g = dn * g_ref[...]
    gx = dn * xh
    ln = inv * (
        g - jnp.mean(g, -1, keepdims=True) - xh * jnp.mean(g * xh, -1, keepdims=True)
    )
    gin_ref[...] = (dy_ref[...].astype(F32) + ln).astype(BF)

    @pl.when(i == 0)
    def _():
        v_ref[...] = jnp.zeros_like(v_ref)

    v_ref[0:1, :] += jnp.sum(gx, 0, keepdims=True)
    v_ref[1:2, :] += jnp.sum(dn, 0, keepdims=True)


def final(ids, x, dy, gain, b_out, ot, dq, dk, dv, acc_o, acc_g, weights, pieces):
    row = pl.BlockSpec((TB, D), lambda i, *_: (i, 0))
    col = pl.BlockSpec((D, TB), lambda i, *_: (0, i))
    vec = pl.BlockSpec((1, D), lambda i, *_: (0, 0))
    wargs = [weights, *pieces]
    return pl.pallas_call(
        functools.partial(final_kernel, len(wargs)),
        grid_spec=pltpu.PrefetchScalarGridSpec(
            num_scalar_prefetch=1,
            grid=(T // TB,),
            in_specs=[
                row,
                row,
                vec,
                vec,
                col,
                col,
                col,
                col,
                row,
                col,
                *[once((w.shape[0], 4 * D)) for w in wargs],
            ],
            out_specs=[row, row, pl.BlockSpec((8, D), lambda i, *_: (0, 0))],
            scratch_shapes=[pltpu.VMEM((D, 4 * D), BF)],
        ),
        out_shape=[
            jax.ShapeDtypeStruct((T, D), BF),
            jax.ShapeDtypeStruct((T, D), BF),
            jax.ShapeDtypeStruct((8, D), F32),
        ],
        compiler_params=params(),
        cost_estimate=cost(8 * T * D * D, 40 * T * D),
    )(ids, x, dy, gain, b_out, ot, dq, dk, dv, acc_o, acc_g, *wargs)


C1 = float(1.0 - np.float32(B1) ** np.float32(STEP))
C2 = float(1.0 - np.float32(B2) ** np.float32(STEP))


def adam_math(g, m, v, w, decay):
    nm = B1 * m + (1.0 - B1) * g
    nv = B2 * v + (1.0 - B2) * g * g
    up = -LR * (nm / C1 / (jnp.sqrt(nv / C2) + ADAM_EPS) + decay * w)
    return nm, nv, up


AC = 512


def adam_kernel(n_alias, ids, sm, rm, so, ro, m_ref, v_ref, w_ref, *refs):
    wg_ref, nm_ref, nv_ref, up_ref = refs[n_alias:]
    summed = pl.program_id(0) == ids[1]
    hr = sm.shape[0]
    mine = jnp.where(summed, sm[...].astype(F32), rm[...].astype(F32))
    other = jnp.where(summed, so[...].astype(F32), ro[...].astype(F32))
    lead = ids[0] == 0
    for h, g in enumerate((jnp.where(lead, mine, other), jnp.where(lead, other, mine))):
        rows = slice(h * hr, (h + 1) * hr)
        nm, nv, up = adam_math(g, m_ref[rows, :], v_ref[rows, :], w_ref[rows, :].astype(F32), DECAY)
        wg_ref[rows, :] = g
        nm_ref[rows, :] = nm
        nv_ref[rows, :] = nv
        up_ref[rows, :] = up


def adam(ids, grads, cols, m, v, w, outs):
    rows, width = m.shape
    hr = rows // 2
    n = grads[0].shape[1]
    pick = lambda hit: pl.BlockSpec(
        (hr, AC), lambda p, j, ids: (0, jnp.where((p == ids[1]) == hit, j, 0))
    )
    b0, b1 = cols[0] // AC, cols[1] // AC
    big = pl.BlockSpec((rows, AC), lambda p, j, ids: (0, jnp.where(p == 0, b0, b1) + j))
    alias = [] if outs is None else list(outs)
    return pl.pallas_call(
        functools.partial(adam_kernel, len(alias)),
        grid_spec=pltpu.PrefetchScalarGridSpec(
            num_scalar_prefetch=1,
            grid=(2, n // AC),
            in_specs=[pick(True), pick(False), pick(True), pick(False), big, big, big]
            + [pl.BlockSpec(memory_space=pl.ANY)] * len(alias),
            out_specs=[big] * 4,
        ),
        out_shape=[jax.ShapeDtypeStruct((rows, width), F32)] * 4,
        input_output_aliases={8 + i: i for i in range(len(alias))},
        compiler_params=pltpu.CompilerParams(
            dimension_semantics=("arbitrary", "arbitrary"), vmem_limit_bytes=VLIM
        ),
        cost_estimate=cost(2 * rows * n * 20, 2 * rows * n * 28),
    )(ids, *grads, m, v, w, *alias)


def after(values, *waits):
    flat = lax.optimization_barrier((*values, *waits))
    return list(flat[: len(values)])


def on_device(shards, reps, hidden_in, cotangent, lengths, weights, moment_m, moment_v, vectors, vector_m, vector_v):
    s = lax.axis_index("shard")
    rep = lax.axis_index("rep")
    c = rep % 2
    z = rep // 2
    zs = reps // 2
    swap = [(i, i ^ 1) for i in range(reps)]
    rows = weights.shape[0]
    hr = rows // 2
    i32 = jnp.int32
    cube = shards == 4 and zs & (zs - 1) == 0 and zs >= 4
    xn = [(i, i ^ 1) for i in range(shards)]
    yn = [(i, i ^ 2) for i in range(shards)]
    zsteps = [3] + [1 << k for k in range(2, 16) if 1 << k < zs]
    zn = lambda bit: [(i, i ^ (2 * bit)) for i in range(reps)]
    own = ((z ^ (z // 2)) % 2) if cube else jnp.int32(0)

    if cube:
        x_order, y_order = (1, 3, 0, 2), (2, 3, 0, 1)
        x_rows = [(s ^ r) * rows for r in x_order]
        y_rows = [(s ^ r) * rows for r in y_order]
        y_in_x = tuple(x_order.index(r) for r in y_order)
    else:
        x_rows = y_rows = [r * rows for r in range(shards)]
        y_in_x = tuple(range(shards))
    cut = lambda at: [b + c * hr for b in at] + [b + (1 - c) * hr for b in at]
    x_off, y_off = cut(x_rows), cut(y_rows)
    stack = lambda *v: jnp.stack([jnp.asarray(x, i32) for x in v])
    length = lengths.astype(i32)
    gain = vectors[:D].reshape(1, D)
    shift = vectors[D : 2 * D].reshape(1, D)
    b_out = vectors[2 * D : 3 * D].reshape(1, D)
    b_in = vectors[3 * D :].reshape(1, FF)
    half_w = lax.dynamic_slice_in_dim(weights, c * hr, hr, 0)

    def part_of(cols):
        return jnp.concatenate([half_w[:, a:b] for a, b in cols], 1)

    q = hr // 2

    def gather_first(part):
        return [lax.ppermute(part, "shard", xn), lax.ppermute(part, "shard", yn)]

    def gather_second(first):
        rx, ry = first
        return [lax.ppermute(rx[:q], "shard", yn), lax.ppermute(ry[q:], "shard", xn)]

    def swapped(mine):
        return mine + [lax.ppermute(p, "rep", swap) for p in mine]

    def gather_whole(part):
        full = lax.all_gather(part, "shard", axis=0, tiled=True)
        other = lax.ppermute(full, "rep", swap)
        return [p[b * hr : (b + 1) * hr] for p in (full, other) for b in range(shards)]

    offsets = [0]
    for size in SIZES:
        offsets.append(offsets[-1] + size)
    apart, fpart = part_of([(0, 4 * D)]), part_of([(4 * D, 4 * D + 2 * FF)])
    if cube:
        base = [(s ^ 1) * rows, (s ^ 2) * rows, (s ^ 3) * rows, (s ^ 3) * rows + q]
        offs = [b + c * hr for b in base] + [b + (1 - c) * hr for b in base]
        one = gather_first(apart)
        one = one + gather_second(one)
        (fpart,) = after([fpart], *one)
        apieces = swapped(one)
        two = gather_first(fpart)
    else:
        offs = cut([b * rows for b in range(shards)])
        apieces = gather_whole(apart)
        two = gather_whole(fpart)
    piece_off = stack(s * rows, *offs)
    len_piece_off = stack(length[0], s * rows, *offs)

    n, nt, dy, dyt, db_out = prep(
        stack(length[0], *x_off), hidden_in, cotangent, gain, shift, hr, shards
    )

    add = lambda *v: sum(x.astype(F32) for x in v).astype(BF)

    class Reduce:
        def __init__(self, mine, theirs, y_first=False):
            self.mine, self.theirs = mine, theirs
            self.ways = (yn, xn) if y_first else (xn, yn)
            self.at = 0
            self.sums = None

        def step(self):
            k, self.at = self.at, self.at + 1
            m = self.mine
            if k == 0:
                sent = self.theirs
                self.got = lax.ppermute(sent, "rep", swap)
            elif not cube:
                if k > 1:
                    return []
                groups = [[2 * j + e for j in range(zs)] for e in range(2)]
                both = add(m, self.got)
                both = lax.psum_scatter(both, "shard", scatter_dimension=1, tiled=True)
                both = lax.psum(both, "rep", axis_index_groups=groups)
                self.sums = (both[0], both[1])
                return []
            elif k == 1:
                sent = add(m[:, : 2 * hr], self.got[:, : 2 * hr])
                self.first = lax.ppermute(sent, "shard", self.ways[0])
                return [sent, self.first]
            elif k == 2:
                sent = add(m[:, 3 * hr :], self.got[:, 3 * hr :], self.first[:, hr:])
                self.second = lax.ppermute(sent, "shard", self.ways[1])
                return [sent, self.second]
            elif k == 3:
                total = add(
                    m[:, 2 * hr : 3 * hr], self.got[:, 2 * hr : 3 * hr], self.first[:, :hr], self.second
                )
                lead = own == 0
                sent = jnp.where(lead, total[1], total[0])
                self.keep = jnp.where(lead, total[0], total[1])
                self.back = lax.ppermute(sent, "rep", zn(1))
                return [sent, self.back]
            elif k <= 3 + len(zsteps):
                self.keep = add(self.keep, self.back)
                self.back = lax.ppermute(self.keep, "rep", zn(zsteps[k - 4]))
                return [self.keep, self.back]
            elif k == 4 + len(zsteps):
                self.keep = add(self.keep, self.back)
                self.back = lax.ppermute(self.keep, "rep", zn(1))
                self.sums = (self.keep, self.back)
                return [self.keep, self.back]
            return [self.theirs, self.got]

        def result(self):
            while self.sums is None:
                self.step()
            return [*self.sums, *[lax.ppermute(v, "rep", swap) for v in self.sums]]

    flight = []

    def turn(values, *steps):
        nonlocal flight
        waits = flight
        flight = []
        for red in steps:
            moved = red.step() if red.sums is None else []
            waits = waits + moved[:1]
            flight = flight + moved[1:]
        return after(values, *waits) if waits else list(values)

    inv_freq = jnp.power(F32(10000.0), -jnp.arange(0, ROT, 2, dtype=F32) / ROT)
    angles = inv_freq[:, None] * jnp.arange(T, dtype=F32)[None, :]
    cos, sin = jnp.cos(angles), jnp.sin(angles)
    qkv, dot_ = proj(piece_off, n, dy, cos, sin, weights, apieces)
    half = HEADS // 2
    heads = attend(length, qkv, dot_, cos, sin, 0, half, None)
    if cube:
        (qkv,) = after([qkv], *two, heads[0])
        three = gather_second(two)
        fpieces = swapped(two)
    ot, dq, dk, dv = attend(length, qkv, dot_, cos, sin, half, half, heads)
    dyg = dy
    if cube:
        (dyg,) = after([dy], ot, *three, *fpieces)
        other = swapped(three)
        fpieces = fpieces[:2] + other[:2] + fpieces[2:] + other[2:]
    else:
        fpieces = two
    reds = [Reduce(*attn_grads(stack(*y_off), nt, dyg, ot, dq, dk, dv, hr, y_in_x), True)]
    places = [(0, 2 * D)]
    reds[0].step()

    acc = None
    dbs = []
    nk = n
    for at, size in zip(offsets, SIZES):
        (nk,) = turn([nk], *reds)
        grads_m, grads_t, db_in, *acc = mlp(
            piece_off, nk, nt, dy, dyt, b_in, weights, fpieces, at, size, acc
        )
        dbs.append(db_in)
        reds.append(Reduce(grads_m, grads_t))
        reds[-1].step()
        places.append((4 * D + at, 4 * D + FF + at))

    (ot,) = turn([ot], *reds)
    out, grad_in, vsum = final(
        len_piece_off, hidden_in, dy, gain, b_out, ot, dq, dk, dv, *acc, weights, apieces
    )
    vec = jnp.concatenate([vsum[0], vsum[1], db_out[0], *[d[0] for d in dbs]])
    if cube:
        vec = vec.reshape(-1, 128)
        vec = vec + lax.ppermute(vec, "rep", swap)
        for way in (xn, yn):
            vec = vec + lax.ppermute(vec, "shard", way)
        for bit in [1] + zsteps:
            vec = vec + lax.ppermute(vec, "rep", zn(bit))
        vec = vec.reshape(-1)
    else:
        vec = lax.psum(vec, ("rep", "shard"))
    core = stack(c, own)
    big = None
    turn([], *reds)
    for i, cols in enumerate(places):
        grads = reds[i].result()
        (moment_m,) = turn([moment_m], *reds[i + 1 :])
        big = adam(core, grads, cols, moment_m, moment_v, weights, big)
    vm, vv, vu = adam_math(vec, vector_m, vector_v, vectors, 0.0)
    return (out, grad_in, *big, vec, vm, vv, vu)


def solution(mesh):
    tok = P(("rep", "shard"), None)
    w = P("shard", None)
    return jax.shard_map(
        functools.partial(on_device, mesh.shape["shard"], mesh.shape["rep"]),
        mesh=mesh,
        in_specs=(tok, tok, P(("rep", "shard")), w, w, w, P(), P(), P()),
        out_specs=(tok, tok, w, w, w, w, P(), P(), P(), P()),
        check_vma=False,
    )
```

time: 1060 us -> 552 us (0.52)
  matrix products: 336 us -> 0 us
  waiting for transfers between devices: 494 us -> 175 us
  Pallas kernels: 0 us -> 246 us
  other arithmetic: 148 us -> 34.7 us
  starting transfers between devices: 0.12 us -> 65.2 us
  blocking collectives: 40.3 us -> 0 us
  between operations: 15.3 us -> 2.45 us
    dot_general x24 -> x0, matrix products: 336 us -> none  [the longest x2 48.9 us: attend_back(): jnp.einsum('qhd,khd->hqk', grad_blk, values, preferred_element_type=jnp.f...]
    pallas_call x0 -> x13, Pallas kernels: none -> 246 us  [the longest x3 90.8 us: mlp(): pl.pallas_call(functools.partial(mlp_kernel, len(wargs), first), grid_spe...]
    all_gather x1 -> x0, waiting for transfers between devices: 227 us -> none  [on_device(): gathered = lax.all_gather(weights, 'shard', axis=0, tiled=True)]
    ppermute x0 -> x53, waiting for transfers between devices: none -> 175 us  [the longest x4 48.1 us: step(): self.first = lax.ppermute(sent, 'shard', self.ways[0])]
    reduce_scatter x1 -> x0, waiting for transfers between devices: 146 us -> none  [on_device(): lax.psum_scatter(weight_terms(pairs).astype(jnp.bfloat16), 'shard', scatt...]
    psum x1 -> x0, waiting for transfers between devices: 120 us -> none  [on_device(): weight_grad = lax.psum(group_rows, 'rep').astype(jnp.float32)]
    ppermute x0 -> x53, starting transfers between devices: none -> 65.2 us  [the longest x4 20 us: step(): self.back = lax.ppermute(self.keep, 'rep', zn(1))]
    psum x1 -> x0, blocking collectives: 40.3 us -> none  [on_device(): vector_grad = lax.psum(vector_local, ('rep', 'shard'))]
  transfers between devices with their start and end apart: 3 -> 53, of which waited for: 3 -> 20; matrix products, arithmetic and copies ran while one was open for 6% -> 9% of each run, Pallas kernels for 0% -> 35%
where the time goes in v1:
time: 552 us; the launch traced here: 543 us
  Pallas kernels  246 us (45%)
  waiting for transfers between devices  175 us (32%)
  starting transfers between devices  65.2 us (12%)
  other arithmetic  34.7 us (6%)
  local copies, waits for them, and re-layouts  19.2 us (3%)
    pallas_call x3, Pallas kernels, mlp(): pl.pallas_call(functools.partial(mlp_kernel, len(wargs), first), grid_spe...  90.8 us
    ppermute x4, waiting for transfers between devices, step(): self.first = lax.ppermute(sent, 'shard', self.ways[0])  48.1 us
    pallas_call x2, Pallas kernels, attend(): pl.pallas_call(functools.partial(attn_kernel, len(alias)), grid_spec=pltp...  47.8 us
    pallas_call x4, Pallas kernels, adam(): pl.pallas_call(functools.partial(adam_kernel, len(alias)), grid_spec=pltp...  42.7 us
    ppermute x4, waiting for transfers between devices, step(): self.back = lax.ppermute(sent, 'rep', zn(1))  34 us
    ppermute x4, waiting for transfers between devices, gather_first(): return [lax.ppermute(part, 'shard', xn), lax.ppermute(part, 'shard', yn)]  32.3 us
    convert_element_type x20, other arithmetic, on_device(): add = lambda *v: sum((x.astype(F32) for x in v)).astype(BF)  31.5 us
    ppermute x4, waiting for transfers between devices, step(): self.back = lax.ppermute(self.keep, 'rep', zn(zsteps[k - 4]))  22.5 us
  transfers between devices with their start and end apart: 53, of which 20 were waited for; matrix products, arithmetic and copies ran while one was open for 9% of the time, Pallas kernels for 35%

profile of v1, /device:TPU:0, one launch (start us, length us, event | category | flops | bytes accessed | tf_op | source)
XLA Modules:
  0.0 542.9 jit_solution(14197395022384712337)
XLA Ops:
  6.5 21.6 %collective-permute-done.refs_1_.refs_10_ = bf16[128,4096]{1,0:T(8,128)(2,1)S(1)} collective-permute-done((bf16[128,4096]{1,0:T(8,128)(2,1)S(1)}, bf16[128,4096]{1,0:T(8,128)(2,1)S(1)}, u32[]{:S(2)}, u32[]{:S(2)}) %collective-permute-start) | collective-permute-done | bytes 1048608 | tf_op jit(solution)/shard_map/ppermute | solution.py:638
  35.7 5.7 %collective-permute-done.2.refs_3_.refs_12_ = bf16[64,4096]{1,0:T(8,128)(2,1)S(1)} collective-permute-done((bf16[64,4096]{1,0:T(8,128)(2,1)S(1)}, bf16[64,4096]{1,0:T(8,128)(2,1)S(1)}, u32[]{:S(2)}, u32[]{:S(2)}) %collective-permute-start.2) | collective-permute-done | bytes 524320 | tf_op jit(solution)/shard_map/ppermute | solution.py:642
  50.1 8.0 %shard_map.168 = (bf16[1024,1024]{1,0:T(8,128)(2,1)}, bf16[1024,1024]{1,0:T(8,128)(2,1)}, bf16[1024,1024]{1,0:T(8,128)(2,1)}, bf16[1024,1024]{1,0:T(8,128)(2,1)}, f32[1,1024]{1,0:T(1,128)}) custom-call(s32[9]{0:T(128)} %stack.89.ids, bf16[1024,1024]{1,0:T(8,128)(2,1)} %x_ref.3, bf16[1024,1024]{1,0:T(8,128)(2,1)} %c_ref.1, f32[1,1024]{1,0:T(1,128)} %bitcast.52, ...), custom_call_target="tpu_custom_call" | custom-call | flops 20971520 | bytes 12582912 | tf_op jit(solution)/shard_map/pallas_call | solution.py:91
  59.9 20.2 %shard_map.169 = (bf16[3072,1024]{1,0:T(8,128)(2,1)}, bf16[1024,1024]{1,0:T(8,128)(2,1)}) custom-call(s32[9]{0:T(128)} %stack.90.ids, bf16[1024,1024]{1,0:T(8,128)(2,1)} %get-tuple-element.99.n_ref, bf16[1024,1024]{1,0:T(8,128)(2,1)} %get-tuple-element.84.d_ref.dy_ref, f32[16,1024]{1,0:T(8,128)} %get-tuple-element.144.cos_ref, ...), custom_call_target="tpu_custom_call" | custom-call | flops 8589934592 | bytes 20971520 | tf_op jit(solution)/shard_map/pallas_call | solution.py:286
  80.2 9.3 %collective-permute-done.8.refs_1_.refs_10_ = bf16[128,8192]{1,0:T(8,128)(2,1)S(1)} collective-permute-done((bf16[128,8192]{1,0:T(8,128)(2,1)}, bf16[128,8192]{1,0:T(8,128)(2,1)S(1)}, u32[]{:S(2)}, u32[]{:S(2)}) %collective-permute-start.8) | collective-permute-done | bytes 2097184 | tf_op jit(solution)/shard_map/ppermute | solution.py:638
  90.8 23.8 %shard_map.170 = (bf16[1024,1024]{1,0:T(8,128)(2,1)}, bf16[1024,1024]{1,0:T(8,128)(2,1)}, bf16[1024,1024]{1,0:T(8,128)(2,1)}, bf16[1024,1024]{1,0:T(8,128)(2,1)}) custom-call(s32[1]{0:T(128)S(6)} %copy.56.len_ref, bf16[3072,1024]{1,0:T(8,128)(2,1)} %get-tuple-element.78.q_ref.k_ref.v_ref, bf16[3072,1024]{1,0:T(8,128)(2,1)} %get-tuple-element.78.q_ref.k_ref.v_ref, ...), custom_call_target="tpu_custom_call" | custom-call | flops 12884901888 | bytes 18874368 | tf_op jit(solution)/shard_map/pallas_call | solution.py:384
  119.4 24.0 %shard_map.171 = (bf16[1024,1024]{1,0:T(8,128)(2,1)}, bf16[1024,1024]{1,0:T(8,128)(2,1)}, bf16[1024,1024]{1,0:T(8,128)(2,1)}, bf16[1024,1024]{1,0:T(8,128)(2,1)}) custom-call(s32[1]{0:T(128)S(6)} %copy.56.len_ref, bf16[3072,1024]{1,0:T(8,128)(2,1)} %get-tuple-element.78.q_ref.k_ref.v_ref, ...), custom_call_target="tpu_custom_call", output_to_operand_aliasing={{0}: (7, {}), {1}: (8, {}), {2}: (9, {}), {3}: (10, {})} | custom-call | flops 12884901888 | bytes 18874368 | tf_op jit(solution)/shard_map/pallas_call | solution.py:384
  144.1 16.9 %shard_map.172 = (bf16[2,512,2048]{2,1,0:T(8,128)(2,1)}, bf16[2,512,2048]{2,1,0:T(8,128)(2,1)}) custom-call(s32[8]{0:T(128)} %stack.91.ids, bf16[1024,1024]{1,0:T(8,128)(2,1)} %get-tuple-element.83.nt_ref, bf16[1024,1024]{1,0:T(8,128)(2,1)} %get-tuple-element.84.d_ref.dy_ref, bf16[1024,1024]{1,0:T(8,128)(2,1)} %get-tuple-element.104.o_ref, ...), custom_call_target="tpu_custom_call" | custom-call | flops 8589934592 | bytes 20971520 | tf_op jit(solution)/shard_map/pallas_call | solution.py:437
  162.3 7.7 %collective-permute-done.14 = bf16[2,512,2048]{2,1,0:T(8,128)(2,1)S(1)} collective-permute-done((bf16[2,512,2048]{2,1,0:T(8,128)(2,1)}, bf16[2,512,2048]{2,1,0:T(8,128)(2,1)S(1)}, u32[]{:S(2)}, u32[]{:S(2)}) %collective-permute-start.14) | collective-permute-done | bytes 4194336 | tf_op jit(solution)/shard_map/ppermute | solution.py:689
  170.0 5.2 add_convert_fusion
  176.5 32.2 %shard_map.173 = (bf16[2,512,1536]{2,1,0:T(8,128)(2,1)}, bf16[2,512,1536]{2,1,0:T(8,128)(2,1)}, f32[1,1536]{1,0:T(1,128)}, f32[1024,1024]{1,0:T(8,128)}, f32[1024,1024]{1,0:T(8,128)}) custom-call(s32[9]{0:T(128)} %stack.90.ids, bf16[1024,1024]{1,0:T(8,128)(2,1)} %get-tuple-element.99.n_ref, bf16[1024,1024]{1,0:T(8,128)(2,1)} %get-tuple-element.83.nt_ref, ...), custom_call_target="tpu_custom_call" | custom-call | flops 19327352832 | bytes 37748736 | tf_op jit(solution)/shard_map/pallas_call | solution.py:206
  210.3 46.7 %collective-permute-done.15 = bf16[2,256,2048]{2,1,0:T(8,128)(2,1)S(1)} collective-permute-done((bf16[2,256,2048]{2,1,0:T(8,128)(2,1)}, bf16[2,256,2048]{2,1,0:T(8,128)(2,1)S(1)}, u32[]{:S(2)}, u32[]{:S(2)}) %collective-permute-start.15) | collective-permute-done | bytes 2097184 | tf_op jit(solution)/shard_map/ppermute | solution.py:701
  263.9 33.3 %shard_map.174 = (bf16[2,512,1536]{2,1,0:T(8,128)(2,1)}, bf16[2,512,1536]{2,1,0:T(8,128)(2,1)}, f32[1,1536]{1,0:T(1,128)}, f32[1024,1024]{1,0:T(8,128)}, f32[1024,1024]{1,0:T(8,128)}) custom-call(s32[9]{0:T(128)} %stack.90.ids, bf16[1024,1024]{1,0:T(8,128)(2,1)} %get-tuple-element.99.n_ref, bf16[1024,1024]{1,0:T(8,128)(2,1)} %get-tuple-element.83.nt_ref, ...), custom_call_target="tpu_custom_call" | custom-call | flops 19327352832 | bytes 37748736 | tf_op jit(solution)/shard_map/pallas_call | solution.py:206
  302.9 11.5 %collective-permute-done.17 = bf16[128,2048]{1,0:T(8,128)(2,1)S(1)} collective-permute-done((bf16[128,2048]{1,0:T(8,128)(2,1)S(1)}, bf16[128,2048]{1,0:T(8,128)(2,1)S(1)}, u32[]{:S(2)}, u32[]{:S(2)}) %collective-permute-start.17) | collective-permute-done | bytes 524320 | tf_op jit(solution)/shard_map/ppermute | solution.py:714
  314.6 3.7 collective-permute-start.33
  318.3 11.8 %collective-permute-done.33 = bf16[128,2048]{1,0:T(8,128)(2,1)S(1)} collective-permute-done((bf16[128,2048]{1,0:T(8,128)(2,1)S(1)}, bf16[128,2048]{1,0:T(8,128)(2,1)S(1)}, u32[]{:S(2)}, u32[]{:S(2)}) %collective-permute-start.33) | collective-permute-done | bytes 524320 | tf_op jit(solution)/shard_map/ppermute | solution.py:718
  330.2 10.9 %collective-permute-start.34 = (bf16[128,2048]{1,0:T(8,128)(2,1)S(1)}, bf16[128,2048]{1,0:T(8,128)(2,1)}, u32[]{:S(2)}, u32[]{:S(2)}) collective-permute-start(bf16[128,2048]{1,0:T(8,128)(2,1)S(1)} %add_convert_fusion.10.sm), channel_id=1, source_target_pairs={{0,8},{4,12},{8,0},{12,4},{16,24},{20,28},{24,16},{28,20},{1,9},{5... | collective-permute-start | bytes 1572872 | tf_op jit(solution)/shard_map/ppermute | solution.py:722
  348.8 25.3 %shard_map.175 = (bf16[2,512,1024]{2,1,0:T(8,128)(2,1)}, bf16[2,512,1024]{2,1,0:T(8,128)(2,1)}, f32[1,1024]{1,0:T(1,128)}, f32[1024,1024]{1,0:T(8,128)}, f32[1024,1024]{1,0:T(8,128)}) custom-call(s32[9]{0:T(128)} %stack.90.ids, bf16[1024,1024]{1,0:T(8,128)(2,1)} %get-tuple-element.99.n_ref, bf16[1024,1024]{1,0:T(8,128)(2,1)} %get-tuple-element.83.nt_ref, ...), custom_call_target="tpu_custom_call" | custom-call | flops 12884901888 | bytes 33554432 | tf_op jit(solution)/shard_map/pallas_call | solution.py:206
  378.2 10.5 %collective-permute-done.35 = bf16[128,1536]{1,0:T(8,128)(2,1)} collective-permute-done((bf16[128,1536]{1,0:T(8,128)(2,1)}, bf16[128,1536]{1,0:T(8,128)(2,1)}, u32[]{:S(2)}, u32[]{:S(2)}) %collective-permute-start.35) | collective-permute-done | bytes 393248 | tf_op jit(solution)/shard_map/ppermute | solution.py:714
  398.0 20.0 %shard_map.176 = (bf16[1024,1024]{1,0:T(8,128)(2,1)}, bf16[1024,1024]{1,0:T(8,128)(2,1)}, f32[8,1024]{1,0:T(8,128)}) custom-call(s32[10]{0:T(128)} %stack.86.ids, bf16[1024,1024]{1,0:T(8,128)(2,1)} %x_ref.3, bf16[1024,1024]{1,0:T(8,128)(2,1)} %get-tuple-element.84.d_ref.dy_ref, f32[1,1024]{1,0:T(1,128)} %bitcast.53, f32[1,1024]{1,0:T(1,128)} %bitcast.54, ...), custom_call_target="tpu_custom_call" | custom-call | flops 8589934592 | bytes 41943040 | tf_op jit(solution)/shard_map/pallas_call | solution.py:503
  427.5 9.1 %collective-permute-done.27 = bf16[2,128,1024]{2,1,0:T(8,128)(2,1)S(1)} collective-permute-done((bf16[2,128,1024]{2,1,0:T(8,128)(2,1)S(1)}, bf16[2,128,1024]{2,1,0:T(8,128)(2,1)S(1)}, u32[]{:S(2)}, u32[]{:S(2)}) %collective-permute-start.27) | collective-permute-done | bytes 524320 | tf_op jit(solution)/shard_map/ppermute | solution.py:705
  439.7 6.5 %collective-permute-done.38 = bf16[128,1536]{1,0:T(8,128)(2,1)S(1)} collective-permute-done((bf16[128,1536]{1,0:T(8,128)(2,1)S(1)}, bf16[128,1536]{1,0:T(8,128)(2,1)S(1)}, u32[]{:S(2)}, u32[]{:S(2)}) %collective-permute-start.38) | collective-permute-done | bytes 393248 | tf_op jit(solution)/shard_map/ppermute | solution.py:714
  449.6 5.6 %collective-permute-done.28 = bf16[128,1024]{1,0:T(8,128)(2,1)S(1)} collective-permute-done((bf16[128,1024]{1,0:T(8,128)(2,1)S(1)}, bf16[128,1024]{1,0:T(8,128)(2,1)S(1)}, u32[]{:S(2)}, u32[]{:S(2)}) %collective-permute-start.28) | collective-permute-done | bytes 262176 | tf_op jit(solution)/shard_map/ppermute | solution.py:714
  455.3 6.5 %collective-permute-done.40 = bf16[128,1536]{1,0:T(8,128)(2,1)S(1)} collective-permute-done((bf16[128,1536]{1,0:T(8,128)(2,1)S(1)}, bf16[128,1536]{1,0:T(8,128)(2,1)S(1)}, u32[]{:S(2)}, u32[]{:S(2)}) %collective-permute-start.40) | collective-permute-done | bytes 393248 | tf_op jit(solution)/shard_map/ppermute | solution.py:718
  465.9 4.2 collective-permute-done.29
  470.1 9.1 %collective-permute-start.41 = (bf16[128,1536]{1,0:T(8,128)(2,1)S(1)}, bf16[128,1536]{1,0:T(8,128)(2,1)S(1)}, u32[]{:S(2)}, u32[]{:S(2)}) collective-permute-start(bf16[128,1536]{1,0:T(8,128)(2,1)S(1)} %add_convert_fusion.13.sm), channel_id=1, source_target_pairs={{0,8},{4,12},{8,0},{12,4},{16,24},{20,28},{24,16},{28,20},{1,9},{5... | collective-permute-start | bytes 1179656 | tf_op jit(solution)/shard_map/ppermute | solution.py:722
  481.4 7.8 %collective-permute-done.51 = f32[56,128]{1,0:T(8,128)S(1)} collective-permute-done((f32[56,128]{1,0:T(8,128)S(1)}, f32[56,128]{1,0:T(8,128)S(1)}, u32[]{:S(2)}, u32[]{:S(2)}) %collective-permute-start.51) | collective-permute-done | bytes 28704 | tf_op jit(solution)/shard_map/ppermute | solution.py:790
  491.2 4.3 collective-permute-done.52
  497.2 13.8 %shard_map.177 = (f32[256,12288]{1,0:T(8,128)}, f32[256,12288]{1,0:T(8,128)}, f32[256,12288]{1,0:T(8,128)}, f32[256,12288]{1,0:T(8,128)}) custom-call(s32[2]{0:T(128)} %pad_add_fusion.ids, bf16[128,2048]{1,0:T(8,128)(2,1)} %copy-done.10, bf16[128,2048]{1,0:T(8,128)(2,1)} %collective-permute-done.34.rm, bf16[128,2048]{1,0:T(8,128)(2,1)} %collective-permute-done.46.so, ...), custom_call_target="tpu_custom_call" | custom-call | flops 20971520 | bytes 29360128 | tf_op jit(solution)/shard_map/pallas_call | solution.py:574
  511.8 10.7 %shard_map.178 = (f32[256,12288]{1,0:T(8,128)}, f32[256,12288]{1,0:T(8,128)}, f32[256,12288]{1,0:T(8,128)}, f32[256,12288]{1,0:T(8,128)}) custom-call(s32[2]{0:T(128)} %pad_add_fusion.ids, bf16[128,1536]{1,0:T(8,128)(2,1)} %copy-done.12, ...), custom_call_target="tpu_custom_call", output_to_operand_aliasing={{0}: (8, {}), {1}: (9, {}), {2}: (10, {}), {3}: (11, {})} | custom-call | flops 15728640 | bytes 22020096 | tf_op jit(solution)/shard_map/pallas_call | solution.py:574
  523.4 10.7 %shard_map.179 = (f32[256,12288]{1,0:T(8,128)}, f32[256,12288]{1,0:T(8,128)}, f32[256,12288]{1,0:T(8,128)}, f32[256,12288]{1,0:T(8,128)}) custom-call(s32[2]{0:T(128)} %pad_add_fusion.ids, bf16[128,1536]{1,0:T(8,128)(2,1)} %copy-done.13, bf16[128,1536]{1,0:T(8,128)(2,1)} %copy-done.23, ...), custom_call_target="tpu_custom_call", output_to_operand_aliasing={{0}: (8, {}), {1}: (9, {}), {2}: (10, {}), {3}: (11, {})} | custom-call | flops 15728640 | bytes 22020096 | tf_op jit(solution)/shard_map/pallas_call | solution.py:574
  534.9 7.5 %shard_map.180 = (f32[256,12288]{1,0:T(8,128)}, f32[256,12288]{1,0:T(8,128)}, f32[256,12288]{1,0:T(8,128)}, f32[256,12288]{1,0:T(8,128)}) custom-call(s32[2]{0:T(128)} %pad_add_fusion.ids, bf16[128,1024]{1,0:T(8,128)(2,1)} %copy-done.19, bf16[128,1024]{1,0:T(8,128)(2,1)} %copy-done.27, ...), custom_call_target="tpu_custom_call", output_to_operand_aliasing={{0}: (8, {}), {1}: (9, {}), {2}: (10, {}), {3}: (11, {})} | custom-call | flops 10485760 | bytes 14680064 | tf_op jit(solution)/shard_map/pallas_call | solution.py:574
  (214 shorter events, 96.5 us)
Async XLA Ops:
  2.0 26.2 %collective-permute-start = (bf16[128,4096]{1,0:T(8,128)(2,1)S(1)}, bf16[128,4096]{1,0:T(8,128)(2,1)S(1)}, u32[]{:S(2)}, u32[]{:S(2)}) collective-permute-start(bf16[128,4096]{1,0:T(8,128)(2,1)S(1)} %constant_dynamic-slice_fusion), channel_id=1, source_target_pairs={{0,1},{1,0},{2,3},{3,2},{4,5},{5,4},{6,7},{7,6},{8,9},{9,8},{10,11... | collective-permute-start | bytes 3145736 | tf_op jit(solution)/shard_map/ppermute | solution.py:638
  5.0 25.0 %collective-permute-start.1 = (bf16[128,4096]{1,0:T(8,128)(2,1)S(1)}, bf16[128,4096]{1,0:T(8,128)(2,1)}, u32[]{:S(2)}, u32[]{:S(2)}) collective-permute-start(bf16[128,4096]{1,0:T(8,128)(2,1)S(1)} %constant_dynamic-slice_fusion), channel_id=1, source_target_pairs={{0,2},{1,3},{2,0},{3,1},{4,6},{5,7},{6,4},{7,5},{8,10},{9,11},{10,... | collective-permute-start | bytes 3145736 | tf_op jit(solution)/shard_map/ppermute | solution.py:638
  43.9 45.6 %collective-permute-start.8 = (bf16[128,8192]{1,0:T(8,128)(2,1)}, bf16[128,8192]{1,0:T(8,128)(2,1)S(1)}, u32[]{:S(2)}, u32[]{:S(2)}) collective-permute-start(bf16[128,8192]{1,0:T(8,128)(2,1)} %dynamic-slice.1), channel_id=1, source_target_pairs={{0,1},{1,0},{2,3},{3,2},{4,5},{5,4},{6,7},{7,6},{8,9},{9,8},{10,11... | collective-permute-start | bytes 6291464 | tf_op jit(solution)/shard_map/ppermute | solution.py:638
  45.4 45.4 %collective-permute-start.9 = (bf16[128,8192]{1,0:T(8,128)(2,1)}, bf16[128,8192]{1,0:T(8,128)(2,1)}, u32[]{:S(2)}, u32[]{:S(2)}) collective-permute-start(bf16[128,8192]{1,0:T(8,128)(2,1)} %dynamic-slice.1), channel_id=1, source_target_pairs={{0,2},{1,3},{2,0},{3,1},{4,6},{5,7},{6,4},{7,5},{8,10},{9,11},{10,... | collective-permute-start | bytes 6291464 | tf_op jit(solution)/shard_map/ppermute | solution.py:638
  89.5 54.6 %collective-permute-start.12 = (bf16[128,8192]{1,0:T(8,128)(2,1)S(1)}, bf16[128,8192]{1,0:T(8,128)(2,1)S(1)}, u32[]{:S(2)}, u32[]{:S(2)}) collective-permute-start(bf16[128,8192]{1,0:T(8,128)(2,1)S(1)} %collective-permute-done.8.refs_1_.refs_10_), channel_id=1, source_target_pairs={{0,4},{4,0},{8,12},{12,8},{16,20},{20,16},{24,28},{28,24},{1,5},{5... | collective-permute-start | bytes 6291464 | tf_op jit(solution)/shard_map/ppermute | solution.py:645
  90.8 53.3 %collective-permute-start.13 = (bf16[128,8192]{1,0:T(8,128)(2,1)}, bf16[128,8192]{1,0:T(8,128)(2,1)}, u32[]{:S(2)}, u32[]{:S(2)}) collective-permute-start(bf16[128,8192]{1,0:T(8,128)(2,1)} %collective-permute-done.9.refs_2_.refs_11_), channel_id=1, source_target_pairs={{0,4},{4,0},{8,12},{12,8},{16,20},{20,16},{24,28},{28,24},{1,5},{5... | collective-permute-start | bytes 6291464 | tf_op jit(solution)/shard_map/ppermute | solution.py:645
  115.6 27.7 %collective-permute-start.10 = (bf16[64,8192]{1,0:T(8,128)(2,1)}, bf16[64,8192]{1,0:T(8,128)(2,1)S(1)}, u32[]{:S(2)}, u32[]{:S(2)}) collective-permute-start(bf16[64,8192]{1,0:T(8,128)(2,1)} %slice.218), channel_id=1, source_target_pairs={{0,2},{1,3},{2,0},{3,1},{4,6},{5,7},{6,4},{7,5},{8,10},{9,11},{10,... | collective-permute-start | bytes 3145736 | tf_op jit(solution)/shard_map/ppermute | solution.py:642
  118.5 25.6 %collective-permute-start.11 = (bf16[64,8192]{1,0:T(8,128)(2,1)}, bf16[64,8192]{1,0:T(8,128)(2,1)}, u32[]{:S(2)}, u32[]{:S(2)}) collective-permute-start(bf16[64,8192]{1,0:T(8,128)(2,1)} %slice.219), channel_id=1, source_target_pairs={{0,1},{1,0},{2,3},{3,2},{4,5},{5,4},{6,7},{7,6},{8,9},{9,8},{10,11... | collective-permute-start | bytes 3145736 | tf_op jit(solution)/shard_map/ppermute | solution.py:642
  208.7 52.3 %collective-permute-start.20 = (bf16[2,512,1536]{2,1,0:T(8,128)(2,1)}, bf16[2,512,1536]{2,1,0:T(8,128)(2,1)}, u32[]{:S(2)}, u32[]{:S(2)}) collective-permute-start(bf16[2,512,1536]{2,1,0:T(8,128)(2,1)} %get-tuple-element.93), channel_id=1, source_target_pairs={{0,4},{4,0},{8,12},{12,8},{16,20},{20,16},{24,28},{28,24},{1,5},{5... | collective-permute-start | bytes 9437192 | tf_op jit(solution)/shard_map/ppermute | solution.py:689
  208.8 48.2 %collective-permute-start.15 = (bf16[2,256,2048]{2,1,0:T(8,128)(2,1)}, bf16[2,256,2048]{2,1,0:T(8,128)(2,1)S(1)}, u32[]{:S(2)}, u32[]{:S(2)}) collective-permute-start(bf16[2,256,2048]{2,1,0:T(8,128)(2,1)} %add_convert_fusion), channel_id=1, source_target_pairs={{0,2},{1,3},{2,0},{3,1},{4,6},{5,7},{6,4},{7,5},{8,10},{9,11},{10,... | collective-permute-start | bytes 6291464 | tf_op jit(solution)/shard_map/ppermute | solution.py:701
  260.1 37.2 %collective-permute-start.16 = (bf16[2,128,2048]{2,1,0:T(8,128)(2,1)}, bf16[2,128,2048]{2,1,0:T(8,128)(2,1)}, u32[]{:S(2)}, u32[]{:S(2)}) collective-permute-start(bf16[2,128,2048]{2,1,0:T(8,128)(2,1)} %add_convert_fusion.5), channel_id=1, source_target_pairs={{0,1},{1,0},{2,3},{3,2},{4,5},{5,4},{6,7},{7,6},{8,9},{9,8},{10,11... | collective-permute-start | bytes 3145736 | tf_op jit(solution)/shard_map/ppermute | solution.py:705
  297.3 48.0 %collective-permute-start.23 = (bf16[2,512,1536]{2,1,0:T(8,128)(2,1)}, bf16[2,512,1536]{2,1,0:T(8,128)(2,1)S(1)}, u32[]{:S(2)}, u32[]{:S(2)}) collective-permute-start(bf16[2,512,1536]{2,1,0:T(8,128)(2,1)} %get-tuple-element.98), channel_id=1, source_target_pairs={{0,4},{4,0},{8,12},{12,8},{16,20},{20,16},{24,28},{28,24},{1,5},{5... | collective-permute-start | bytes 9437192 | tf_op jit(solution)/shard_map/ppermute | solution.py:689
  301.8 39.4 %collective-permute-start.21 = (bf16[2,256,1536]{2,1,0:T(8,128)(2,1)S(1)}, bf16[2,256,1536]{2,1,0:T(8,128)(2,1)S(1)}, u32[]{:S(2)}, u32[]{:S(2)}) collective-permute-start(bf16[2,256,1536]{2,1,0:T(8,128)(2,1)S(1)} %copy-done.14), channel_id=1, source_target_pairs={{0,1},{1,0},{2,3},{3,2},{4,5},{5,4},{6,7},{7,6},{8,9},{9,8},{10,11... | collective-permute-start | bytes 4718600 | tf_op jit(solution)/shard_map/ppermute | solution.py:701
  330.2 47.9 %collective-permute-start.34 = (bf16[128,2048]{1,0:T(8,128)(2,1)S(1)}, bf16[128,2048]{1,0:T(8,128)(2,1)}, u32[]{:S(2)}, u32[]{:S(2)}) collective-permute-start(bf16[128,2048]{1,0:T(8,128)(2,1)S(1)} %add_convert_fusion.10.sm), channel_id=1, source_target_pairs={{0,8},{4,12},{8,0},{12,4},{16,24},{20,28},{24,16},{28,20},{1,9},{5... | collective-permute-start | bytes 1572872 | tf_op jit(solution)/shard_map/ppermute | solution.py:722
  344.0 30.3 %collective-permute-start.22 = (bf16[2,128,1536]{2,1,0:T(8,128)(2,1)}, bf16[2,128,1536]{2,1,0:T(8,128)(2,1)S(1)}, u32[]{:S(2)}, u32[]{:S(2)}) collective-permute-start(bf16[2,128,1536]{2,1,0:T(8,128)(2,1)} %add_convert_fusion.9), channel_id=1, source_target_pairs={{0,2},{1,3},{2,0},{3,1},{4,6},{5,7},{6,4},{7,5},{8,10},{9,11},{10,... | collective-permute-start | bytes 2359304 | tf_op jit(solution)/shard_map/ppermute | solution.py:705
  347.5 44.9 %collective-permute-start.24 = (bf16[2,256,1536]{2,1,0:T(8,128)(2,1)}, bf16[2,256,1536]{2,1,0:T(8,128)(2,1)}, u32[]{:S(2)}, u32[]{:S(2)}) collective-permute-start(bf16[2,256,1536]{2,1,0:T(8,128)(2,1)} %add_convert_fusion.1), channel_id=1, source_target_pairs={{0,1},{1,0},{2,3},{3,2},{4,5},{5,4},{6,7},{7,6},{8,9},{9,8},{10,11... | collective-permute-start | bytes 4718600 | tf_op jit(solution)/shard_map/ppermute | solution.py:701
  374.2 21.6 %collective-permute-start.25 = (bf16[2,512,1024]{2,1,0:T(8,128)(2,1)}, bf16[2,512,1024]{2,1,0:T(8,128)(2,1)S(1)}, u32[]{:S(2)}, u32[]{:S(2)}) collective-permute-start(bf16[2,512,1024]{2,1,0:T(8,128)(2,1)} %get-tuple-element.103), channel_id=1, source_target_pairs={{0,4},{4,0},{8,12},{12,8},{16,20},{20,16},{24,28},{28,24},{1,5},{5... | collective-permute-start | bytes 6291464 | tf_op jit(solution)/shard_map/ppermute | solution.py:689
  377.6 86.8 %collective-permute-start.46 = (bf16[128,2048]{1,0:T(8,128)(2,1)S(1)}, bf16[128,2048]{1,0:T(8,128)(2,1)}, u32[]{:S(2)}, u32[]{:S(2)}) collective-permute-start(bf16[128,2048]{1,0:T(8,128)(2,1)S(1)} %add_convert_fusion.10.sm), channel_id=1, source_target_pairs={{0,4},{4,0},{8,12},{12,8},{16,20},{20,16},{24,28},{28,24},{1,5},{5... | collective-permute-start | bytes 1572872 | tf_op jit(solution)/shard_map/ppermute | solution.py:730
  378.1 101.2 %collective-permute-start.47 = (bf16[128,2048]{1,0:T(8,128)(2,1)}, bf16[128,2048]{1,0:T(8,128)(2,1)}, u32[]{:S(2)}, u32[]{:S(2)}) collective-permute-start(bf16[128,2048]{1,0:T(8,128)(2,1)} %collective-permute-done.34.rm), channel_id=1, source_target_pairs={{0,4},{4,0},{8,12},{12,8},{16,20},{20,16},{24,28},{28,24},{1,5},{5... | collective-permute-start | bytes 1572872 | tf_op jit(solution)/shard_map/ppermute | solution.py:730
  389.8 29.1 %collective-permute-start.36 = (bf16[128,1536]{1,0:T(8,128)(2,1)S(1)}, bf16[128,1536]{1,0:T(8,128)(2,1)S(1)}, u32[]{:S(2)}, u32[]{:S(2)}) collective-permute-start(bf16[128,1536]{1,0:T(8,128)(2,1)S(1)} %fusion.2), channel_id=1, source_target_pairs={{0,24},{4,28},{8,16},{12,20},{16,8},{20,12},{24,0},{28,4},{1,25},{... | collective-permute-start | bytes 1179656 | tf_op jit(solution)/shard_map/ppermute | solution.py:718
  395.2 28.7 %collective-permute-start.37 = (bf16[2,128,1536]{2,1,0:T(8,128)(2,1)}, bf16[2,128,1536]{2,1,0:T(8,128)(2,1)}, u32[]{:S(2)}, u32[]{:S(2)}) collective-permute-start(bf16[2,128,1536]{2,1,0:T(8,128)(2,1)} %add_convert_fusion.7), channel_id=1, source_target_pairs={{0,2},{1,3},{2,0},{3,1},{4,6},{5,7},{6,4},{7,5},{8,10},{9,11},{10,... | collective-permute-start | bytes 2359304 | tf_op jit(solution)/shard_map/ppermute | solution.py:705
  397.2 24.5 %collective-permute-start.26 = (bf16[2,256,1024]{2,1,0:T(8,128)(2,1)}, bf16[2,256,1024]{2,1,0:T(8,128)(2,1)}, u32[]{:S(2)}, u32[]{:S(2)}) collective-permute-start(bf16[2,256,1024]{2,1,0:T(8,128)(2,1)} %add_convert_fusion.3), channel_id=1, source_target_pairs={{0,1},{1,0},{2,3},{3,2},{4,5},{5,4},{6,7},{7,6},{8,9},{9,8},{10,11... | collective-permute-start | bytes 3145736 | tf_op jit(solution)/shard_map/ppermute | solution.py:701
  420.2 61.2 %collective-permute-start.39 = (bf16[128,1536]{1,0:T(8,128)(2,1)S(1)}, bf16[128,1536]{1,0:T(8,128)(2,1)}, u32[]{:S(2)}, u32[]{:S(2)}) collective-permute-start(bf16[128,1536]{1,0:T(8,128)(2,1)S(1)} %add_convert_fusion.14.sm), channel_id=1, source_target_pairs={{0,8},{4,12},{8,0},{12,4},{16,24},{20,28},{24,16},{28,20},{1,9},{5... | collective-permute-start | bytes 1179656 | tf_op jit(solution)/shard_map/ppermute | solution.py:722
  421.7 26.5 %collective-permute-start.49 = (f32[56,128]{1,0:T(8,128)S(1)}, f32[56,128]{1,0:T(8,128)S(1)}, u32[]{:S(2)}, u32[]{:S(2)}) collective-permute-start(f32[56,128]{1,0:T(8,128)S(1)} %bitcast_add_fusion), channel_id=1, source_target_pairs={{0,1},{1,0},{2,3},{3,2},{4,5},{5,4},{6,7},{7,6},{8,9},{9,8},{10,11... | collective-permute-start | bytes 86024 | tf_op jit(solution)/shard_map/ppermute | solution.py:788
  455.2 34.5 %collective-permute-start.44 = (bf16[128,1536]{1,0:T(8,128)(2,1)S(1)}, bf16[128,1536]{1,0:T(8,128)(2,1)S(1)}, u32[]{:S(2)}, u32[]{:S(2)}) collective-permute-start(bf16[128,1536]{1,0:T(8,128)(2,1)S(1)} %add_convert_fusion.14.sm), channel_id=1, source_target_pairs={{0,4},{4,0},{8,12},{12,8},{16,20},{20,16},{24,28},{28,24},{1,5},{5... | collective-permute-start | bytes 1179656 | tf_op jit(solution)/shard_map/ppermute | solution.py:730
  470.1 19.1 %collective-permute-start.41 = (bf16[128,1536]{1,0:T(8,128)(2,1)S(1)}, bf16[128,1536]{1,0:T(8,128)(2,1)S(1)}, u32[]{:S(2)}, u32[]{:S(2)}) collective-permute-start(bf16[128,1536]{1,0:T(8,128)(2,1)S(1)} %add_convert_fusion.13.sm), channel_id=1, source_target_pairs={{0,8},{4,12},{8,0},{12,4},{16,24},{20,28},{24,16},{28,20},{1,9},{5... | collective-permute-start | bytes 1179656 | tf_op jit(solution)/shard_map/ppermute | solution.py:722
  479.2 16.2 %collective-permute-start.30 = (bf16[128,1024]{1,0:T(8,128)(2,1)S(1)}, bf16[128,1024]{1,0:T(8,128)(2,1)S(1)}, u32[]{:S(2)}, u32[]{:S(2)}) collective-permute-start(bf16[128,1024]{1,0:T(8,128)(2,1)S(1)} %add_convert_fusion.15.sm), channel_id=1, source_target_pairs={{0,8},{4,12},{8,0},{12,4},{16,24},{20,28},{24,16},{28,20},{1,9},{5... | collective-permute-start | bytes 786440 | tf_op jit(solution)/shard_map/ppermute | solution.py:722
  481.4 29.6 %collective-permute-start.45 = (bf16[128,1536]{1,0:T(8,128)(2,1)}, bf16[128,1536]{1,0:T(8,128)(2,1)S(1)}, u32[]{:S(2)}, u32[]{:S(2)}) collective-permute-start(bf16[128,1536]{1,0:T(8,128)(2,1)} %collective-permute-done.39.rm), channel_id=1, source_target_pairs={{0,4},{4,0},{8,12},{12,8},{16,20},{20,16},{24,28},{28,24},{1,5},{5... | collective-permute-start | bytes 1179656 | tf_op jit(solution)/shard_map/ppermute | solution.py:730
  489.2 33.3 %collective-permute-start.42 = (bf16[128,1536]{1,0:T(8,128)(2,1)S(1)}, bf16[128,1536]{1,0:T(8,128)(2,1)S(1)}, u32[]{:S(2)}, u32[]{:S(2)}) collective-permute-start(bf16[128,1536]{1,0:T(8,128)(2,1)S(1)} %add_convert_fusion.13.sm), channel_id=1, source_target_pairs={{0,4},{4,0},{8,12},{12,8},{16,20},{20,16},{24,28},{28,24},{1,5},{5... | collective-permute-start | bytes 1179656 | tf_op jit(solution)/shard_map/ppermute | solution.py:730
  489.2 33.3 %collective-permute-start.43 = (bf16[128,1536]{1,0:T(8,128)(2,1)S(1)}, bf16[128,1536]{1,0:T(8,128)(2,1)S(1)}, u32[]{:S(2)}, u32[]{:S(2)}) collective-permute-start(bf16[128,1536]{1,0:T(8,128)(2,1)S(1)} %collective-permute-done.41.rm), channel_id=1, source_target_pairs={{0,4},{4,0},{8,12},{12,8},{16,20},{20,16},{24,28},{28,24},{1,5},{5... | collective-permute-start | bytes 1179656 | tf_op jit(solution)/shard_map/ppermute | solution.py:730
  495.5 38.6 %collective-permute-start.31 = (bf16[128,1024]{1,0:T(8,128)(2,1)S(1)}, bf16[128,1024]{1,0:T(8,128)(2,1)S(1)}, u32[]{:S(2)}, u32[]{:S(2)}) collective-permute-start(bf16[128,1024]{1,0:T(8,128)(2,1)S(1)} %add_convert_fusion.15.sm), channel_id=1, source_target_pairs={{0,4},{4,0},{8,12},{12,8},{16,20},{20,16},{24,28},{28,24},{1,5},{5... | collective-permute-start | bytes 786440 | tf_op jit(solution)/shard_map/ppermute | solution.py:730
  495.5 38.6 %collective-permute-start.32 = (bf16[128,1024]{1,0:T(8,128)(2,1)S(1)}, bf16[128,1024]{1,0:T(8,128)(2,1)S(1)}, u32[]{:S(2)}, u32[]{:S(2)}) collective-permute-start(bf16[128,1024]{1,0:T(8,128)(2,1)S(1)} %collective-permute-done.30.rm), channel_id=1, source_target_pairs={{0,4},{4,0},{8,12},{12,8},{16,20},{20,16},{24,28},{28,24},{1,5},{5... | collective-permute-start | bytes 786440 | tf_op jit(solution)/shard_map/ppermute | solution.py:730
  (58 other events, 882.4 us)

commit v2 on v1

--- a/solution.py
+++ b/solution.py
@@ -35,7 +35,7 @@
 TN = (((0,), (0,)), ((), ()))
 TT = (((0,), (1,)), ((), ()))
 TILE = 512
-SIZES = (1536, 1536, 1024)
+SIZES = (2048, 1024, 1024)
 MB = 1024
 TB = 256
 
@@ -54,10 +54,8 @@
     return pl.BlockSpec(shape, lambda *_: (0,) * len(shape), pipeline_mode=pl.Buffered(1))
 
 
-def cost(flops, nbytes, trans=0):
-    return pl.CostEstimate(
-        flops=int(flops), bytes_accessed=int(nbytes), transcendentals=int(trans)
-    )
+def cost(us):
+    return pl.CostEstimate(flops=int(us * 1.15e9), bytes_accessed=1024, transcendentals=0)
 
 
 def prep_kernel(hr, blocks, ids, x_ref, c_ref, g_ref, b_ref, n_ref, nt_ref, d_ref, dt_ref, db_ref, s_ref):
@@ -116,7 +114,7 @@
             jax.ShapeDtypeStruct((1, D), F32),
         ],
         compiler_params=params(),
-        cost_estimate=cost(T * D * 20, T * D * 12),
+        cost_estimate=cost(8),
     )(ids, x, cot, gain, shift)
 
 
@@ -239,7 +237,7 @@
             jax.ShapeDtypeStruct((D, T), F32),
         ],
         compiler_params=params(),
-        cost_estimate=cost(12 * T * D * size, 8 * D * size + 24 * T * D, T * size),
+        cost_estimate=cost(43 * size / 2048),
     )(ids, n, nt, dy, dyt, bias, *wargs, *wargs, *([] if first else acc))
 
 
@@ -310,7 +308,7 @@
             jax.ShapeDtypeStruct((D, T), BF),
         ],
         compiler_params=params(),
-        cost_estimate=cost(8 * T * D * D, 20 * T * D),
+        cost_estimate=cost(20),
     )(ids, n, dy, cos, sin, *wargs, *wargs)
 
 
@@ -400,7 +398,7 @@
         out_shape=[shape] * 4,
         input_output_aliases={7 + i: i for i in range(len(alias))},
         compiler_params=params(),
-        cost_estimate=cost(12 * T * T * D, 18 * T * D, T * T * HEADS // 2),
+        cost_estimate=cost(46 * heads / HEADS),
     )(length, qkv, qkv, qkv, dot_, cos, sin, *alias)
 
 
@@ -452,7 +450,7 @@
         ),
         out_shape=[gshape] * 2,
         compiler_params=params(),
-        cost_estimate=cost(8 * T * D * D, 20 * T * D),
+        cost_estimate=cost(17),
     )(ids, nt, dy, ot, dq, dk, dv)
 
 
@@ -527,7 +525,7 @@
             jax.ShapeDtypeStruct((8, D), F32),
         ],
         compiler_params=params(),
-        cost_estimate=cost(8 * T * D * D, 40 * T * D),
+        cost_estimate=cost(20),
     )(ids, x, dy, gain, b_out, ot, dq, dk, dv, acc_o, acc_g, *wargs)
 
 
@@ -542,7 +540,7 @@
     return nm, nv, up
 
 
-AC = 512
+AC = 1024
 
 
 def adam_kernel(n_alias, ids, sm, rm, so, ro, m_ref, v_ref, w_ref, *refs):
@@ -585,7 +583,7 @@
         compiler_params=pltpu.CompilerParams(
             dimension_semantics=("arbitrary", "arbitrary"), vmem_limit_bytes=VLIM
         ),
-        cost_estimate=cost(2 * rows * n * 20, 2 * rows * n * 28),
+        cost_estimate=cost(12 * n / 2048),
     )(ids, *grads, m, v, w, *alias)
 
 
@@ -629,6 +627,10 @@
     b_in = vectors[3 * D :].reshape(1, FF)
     half_w = lax.dynamic_slice_in_dim(weights, c * hr, hr, 0)
 
+    n, nt, dy, dyt, db_out = prep(
+        stack(length[0], *x_off), hidden_in, cotangent, gain, shift, hr, shards
+    )
+
     def part_of(cols):
         return jnp.concatenate([half_w[:, a:b] for a, b in cols], 1)
 
@@ -657,6 +659,7 @@
         base = [(s ^ 1) * rows, (s ^ 2) * rows, (s ^ 3) * rows, (s ^ 3) * rows + q]
         offs = [b + c * hr for b in base] + [b + (1 - c) * hr for b in base]
         one = gather_first(apart)
+        one = after(one, n)
         one = one + gather_second(one)
         (fpart,) = after([fpart], *one)
         apieces = swapped(one)
@@ -668,61 +671,60 @@
     piece_off = stack(s * rows, *offs)
     len_piece_off = stack(length[0], s * rows, *offs)
 
-    n, nt, dy, dyt, db_out = prep(
-        stack(length[0], *x_off), hidden_in, cotangent, gain, shift, hr, shards
-    )
-
     add = lambda *v: sum(x.astype(F32) for x in v).astype(BF)
+
+    cuts = 4
 
     class Reduce:
         def __init__(self, mine, theirs, y_first=False):
-            self.mine, self.theirs = mine, theirs
+            self.mine = mine
             self.ways = (yn, xn) if y_first else (xn, yn)
             self.at = 0
             self.sums = None
+            h = mine.shape[1] // (cuts // 2)
+            self.got = [
+                [lax.ppermute(theirs[e, b * h : (b + 1) * h], "rep", swap) for e in range(2)]
+                for b in range(cuts // 2)
+            ]
+            self.brought = None
+
+        def settle(self, last):
+            if self.brought is not None:
+                (self.brought,) = after([self.brought], last)
 
         def step(self):
-            k, self.at = self.at, self.at + 1
+            self.at += 1
+            k = self.at
             m = self.mine
-            if k == 0:
-                sent = self.theirs
-                self.got = lax.ppermute(sent, "rep", swap)
-            elif not cube:
-                if k > 1:
-                    return []
+            near, far = [jnp.stack(v) for v in self.got]
+            if not cube:
                 groups = [[2 * j + e for j in range(zs)] for e in range(2)]
-                both = add(m, self.got)
+                both = add(m, jnp.concatenate([near, far], 1))
                 both = lax.psum_scatter(both, "shard", scatter_dimension=1, tiled=True)
                 both = lax.psum(both, "rep", axis_index_groups=groups)
                 self.sums = (both[0], both[1])
                 return []
-            elif k == 1:
-                sent = add(m[:, : 2 * hr], self.got[:, : 2 * hr])
-                self.first = lax.ppermute(sent, "shard", self.ways[0])
-                return [sent, self.first]
+            if k == 1:
+                sent = add(m[:, : 2 * hr], near)
+                self.brought = lax.ppermute(sent, "shard", self.ways[0])
             elif k == 2:
-                sent = add(m[:, 3 * hr :], self.got[:, 3 * hr :], self.first[:, hr:])
-                self.second = lax.ppermute(sent, "shard", self.ways[1])
-                return [sent, self.second]
+                self.first = self.brought
+                sent = add(m[:, 3 * hr :], far[:, hr:], self.first[:, hr:])
+                self.brought = lax.ppermute(sent, "shard", self.ways[1])
             elif k == 3:
-                total = add(
-                    m[:, 2 * hr : 3 * hr], self.got[:, 2 * hr : 3 * hr], self.first[:, :hr], self.second
-                )
+                total = add(m[:, 2 * hr : 3 * hr], far[:, :hr], self.first[:, :hr], self.brought)
                 lead = own == 0
                 sent = jnp.where(lead, total[1], total[0])
                 self.keep = jnp.where(lead, total[0], total[1])
-                self.back = lax.ppermute(sent, "rep", zn(1))
-                return [sent, self.back]
+                self.brought = lax.ppermute(sent, "rep", zn(1))
             elif k <= 3 + len(zsteps):
-                self.keep = add(self.keep, self.back)
-                self.back = lax.ppermute(self.keep, "rep", zn(zsteps[k - 4]))
-                return [self.keep, self.back]
-            elif k == 4 + len(zsteps):
-                self.keep = add(self.keep, self.back)
-                self.back = lax.ppermute(self.keep, "rep", zn(1))
-                self.sums = (self.keep, self.back)
-                return [self.keep, self.back]
-            return [self.theirs, self.got]
+                sent = self.keep = add(self.keep, self.brought)
+                self.brought = lax.ppermute(sent, "rep", zn(zsteps[k - 4]))
+            else:
+                sent = self.keep = add(self.keep, self.brought)
+                self.brought = lax.ppermute(sent, "rep", zn(1))
+                self.sums = (sent, self.brought)
+            return [sent, self.brought]
 
         def result(self):
             while self.sums is None:
@@ -731,14 +733,16 @@
 
     flight = []
 
-    def turn(values, *steps):
+    def turn(values, last, *steps):
         nonlocal flight
         waits = flight
         flight = []
         for red in steps:
-            moved = red.step() if red.sums is None else []
-            waits = waits + moved[:1]
-            flight = flight + moved[1:]
+            if red.sums is None:
+                red.settle(last)
+                moved = red.step()
+                waits = waits + moved[:1]
+                flight = flight + moved[1:]
         return after(values, *waits) if waits else list(values)
 
     inv_freq = jnp.power(F32(10000.0), -jnp.arange(0, ROT, 2, dtype=F32) / ROT)
@@ -748,7 +752,7 @@
     half = HEADS // 2
     heads = attend(length, qkv, dot_, cos, sin, 0, half, None)
     if cube:
-        (qkv,) = after([qkv], *two, heads[0])
+        *two, qkv = after([*two, qkv], heads[0])
         three = gather_second(two)
         fpieces = swapped(two)
     ot, dq, dk, dv = attend(length, qkv, dot_, cos, sin, half, half, heads)
@@ -761,22 +765,19 @@
         fpieces = two
     reds = [Reduce(*attn_grads(stack(*y_off), nt, dyg, ot, dq, dk, dv, hr, y_in_x), True)]
     places = [(0, 2 * D)]
-    reds[0].step()
-
     acc = None
     dbs = []
     nk = n
     for at, size in zip(offsets, SIZES):
-        (nk,) = turn([nk], *reds)
+        (nk,) = turn([nk], dbs[-1] if dbs else dv, *reds)
         grads_m, grads_t, db_in, *acc = mlp(
             piece_off, nk, nt, dy, dyt, b_in, weights, fpieces, at, size, acc
         )
         dbs.append(db_in)
         reds.append(Reduce(grads_m, grads_t))
-        reds[-1].step()
         places.append((4 * D + at, 4 * D + FF + at))
 
-    (ot,) = turn([ot], *reds)
+    (ot,) = turn([ot], dbs[-1], *reds)
     out, grad_in, vsum = final(
         len_piece_off, hidden_in, dy, gain, b_out, ot, dq, dk, dv, *acc, weights, apieces
     )
@@ -793,11 +794,13 @@
         vec = lax.psum(vec, ("rep", "shard"))
     core = stack(c, own)
     big = None
-    turn([], *reds)
+    last = vsum
+    turn([], last, *reds)
     for i, cols in enumerate(places):
         grads = reds[i].result()
-        (moment_m,) = turn([moment_m], *reds[i + 1 :])
+        (moment_m,) = turn([moment_m], last, *reds[i + 1 :])
         big = adam(core, grads, cols, moment_m, moment_v, weights, big)
+        last = big[0][:8, :128]
     vm, vv, vu = adam_math(vec, vector_m, vector_v, vectors, 0.0)
     return (out, grad_in, *big, vec, vm, vv, vu)
 

time: 552 us -> 502 us (0.909)
  waiting for transfers between devices: 175 us -> 115 us
  local copies, waits for them, and re-layouts: 19.2 us -> 31.7 us
    ppermute x24 -> x36, waiting for transfers between devices: 121 us -> 76.8 us  [the longest x8 30.6 us: step(): self.brought = lax.ppermute(sent, 'rep', zn(1))]
    ppermute x4, waiting for transfers between devices: 32.3 us -> 16.6 us  [gather_first(): return [lax.ppermute(part, 'shard', xn), lax.ppermute(part, 'shard', yn)]]
    squeeze x0 -> x4, local copies, waits for them, and re-layouts: none -> 13.9 us  [__init__(): theirs[e, b * h:(b + 1) * h]]
    ppermute x2, waiting for transfers between devices: 2.35 us -> 9.15 us  [gather_second(): lax.ppermute(ry[q:], 'shard', xn)]
    ppermute x24 -> x36, starting transfers between devices: 44.6 us -> 51.2 us  [the longest x4 25.2 us: step(): self.brought = lax.ppermute(sent, 'rep', zn(zsteps[k - 4]))]
  transfers between devices with their start and end apart: 53 -> 65, of which waited for: 20 -> 24; matrix products, arithmetic and copies ran while one was open for 9% -> 11% of each run, Pallas kernels for 35% -> 44%
where the time goes in v2:
time: 502 us; the launch traced here: 493 us
  Pallas kernels  241 us (48%)
  waiting for transfers between devices  115 us (23%)
  starting transfers between devices  67 us (13%)
  other arithmetic  36.1 us (7%)
  local copies, waits for them, and re-layouts  31.7 us (6%)
    pallas_call x3, Pallas kernels, mlp(): pl.pallas_call(functools.partial(mlp_kernel, len(wargs), first), grid_spe...  90.6 us
    pallas_call x2, Pallas kernels, attend(): pl.pallas_call(functools.partial(attn_kernel, len(alias)), grid_spec=pltp...  47.8 us
    pallas_call x4, Pallas kernels, adam(): pl.pallas_call(functools.partial(adam_kernel, len(alias)), grid_spec=pltp...  37.4 us
    convert_element_type x20, other arithmetic, on_device(): add = lambda *v: sum((x.astype(F32) for x in v)).astype(BF)  32.1 us
    ppermute x8, waiting for transfers between devices, step(): self.brought = lax.ppermute(sent, 'rep', zn(1))  30.6 us
    ppermute x4, waiting for transfers between devices, step(): self.brought = lax.ppermute(sent, 'shard', self.ways[1])  25.8 us
    ppermute x4, starting transfers between devices, step(): self.brought = lax.ppermute(sent, 'rep', zn(zsteps[k - 4]))  25.2 us
    pallas_call x1, Pallas kernels, proj(): pl.pallas_call(functools.partial(proj_kernel, len(wargs)), grid_spec=pltp...  20.3 us
  transfers between devices with their start and end apart: 65, of which 24 were waited for; matrix products, arithmetic and copies ran while one was open for 11% of the time, Pallas kernels for 44%

profile of v2, /device:TPU:0, one launch (start us, length us, event | category | flops | bytes accessed | tf_op | source)
XLA Modules:
  0.0 493.1 jit_solution(1773872423746528749)
XLA Ops:
  2.0 3.0 collective-permute-start.1
  8.4 8.0 %shard_map.168 = (bf16[1024,1024]{1,0:T(8,128)(2,1)}, bf16[1024,1024]{1,0:T(8,128)(2,1)}, bf16[1024,1024]{1,0:T(8,128)(2,1)}, bf16[1024,1024]{1,0:T(8,128)(2,1)}, f32[1,1024]{1,0:T(1,128)}) custom-call(s32[9]{0:T(128)} %stack.173.ids, bf16[1024,1024]{1,0:T(8,128)(2,1)} %x_ref.3, bf16[1024,1024]{1,0:T(8,128)(2,1)} %c_ref.1, f32[1,1024]{1,0:T(1,128)} %bitcast.129, ...), custom_call_target="tpu_custom_call" | custom-call | flops 9200000000 | bytes 1024 | tf_op jit(solution)/shard_map/pallas_call | solution.py:89
  16.3 11.8 %collective-permute-done.1.refs_2_.refs_11_ = bf16[128,4096]{1,0:T(8,128)(2,1)S(1)} collective-permute-done((bf16[128,4096]{1,0:T(8,128)(2,1)S(1)}, bf16[128,4096]{1,0:T(8,128)(2,1)S(1)}, u32[]{:S(2)}, u32[]{:S(2)}) %collective-permute-start.1) | collective-permute-done | bytes 1048608 | tf_op jit(solution)/shard_map/ppermute | solution.py:640
  33.5 8.9 %collective-permute-done.3.refs_4_.refs_13_ = bf16[64,4096]{1,0:T(8,128)(2,1)} collective-permute-done((bf16[64,4096]{1,0:T(8,128)(2,1)S(1)}, bf16[64,4096]{1,0:T(8,128)(2,1)}, u32[]{:S(2)}, u32[]{:S(2)}) %collective-permute-start.3) | collective-permute-done | bytes 524320 | tf_op jit(solution)/shard_map/ppermute | solution.py:644
  50.0 20.3 %shard_map.169 = (bf16[3072,1024]{1,0:T(8,128)(2,1)}, bf16[1024,1024]{1,0:T(8,128)(2,1)}) custom-call(s32[9]{0:T(128)} %stack.174.ids, bf16[1024,1024]{1,0:T(8,128)(2,1)} %get-tuple-element.127.n_ref, bf16[1024,1024]{1,0:T(8,128)(2,1)} %get-tuple-element.107.d_ref.dy_ref, f32[16,1024]{1,0:T(8,128)} %get-tuple-element.198.cos_ref, ...), custom_call_target="tpu_custom_call" | custom-call | flops 23000000512 | bytes 1024 | tf_op jit(solution)/shard_map/pallas_call | solution.py:284
  70.3 23.8 %shard_map.170 = (bf16[1024,1024]{1,0:T(8,128)(2,1)}, bf16[1024,1024]{1,0:T(8,128)(2,1)}, bf16[1024,1024]{1,0:T(8,128)(2,1)}, bf16[1024,1024]{1,0:T(8,128)(2,1)}) custom-call(s32[1]{0:T(128)S(6)} %copy.56.len_ref, bf16[3072,1024]{1,0:T(8,128)(2,1)} %get-tuple-element.99.q_ref.k_ref.v_ref, bf16[3072,1024]{1,0:T(8,128)(2,1)} %get-tuple-element.99.q_ref.k_ref.v_ref, ...), custom_call_target="tpu_custom_call" | custom-call | flops 26449999872 | bytes 1024 | tf_op jit(solution)/shard_map/pallas_call | solution.py:382
  101.5 24.0 %shard_map.171 = (bf16[1024,1024]{1,0:T(8,128)(2,1)}, bf16[1024,1024]{1,0:T(8,128)(2,1)}, bf16[1024,1024]{1,0:T(8,128)(2,1)}, bf16[1024,1024]{1,0:T(8,128)(2,1)}) custom-call(s32[1]{0:T(128)S(6)} %copy.56.len_ref, bf16[3072,1024]{1,0:T(8,128)(2,1)} %get-tuple-element.99.q_ref.k_ref.v_ref, ...), custom_call_target="tpu_custom_call", output_to_operand_aliasing={{0}: (7, {}), {1}: (8, {}), {2}: (9, {}), {3}: (10, {})} | custom-call | flops 26449999872 | bytes 1024 | tf_op jit(solution)/shard_map/pallas_call | solution.py:382
  126.1 16.9 %shard_map.172 = (bf16[2,512,2048]{2,1,0:T(8,128)(2,1)}, bf16[2,512,2048]{2,1,0:T(8,128)(2,1)}) custom-call(s32[8]{0:T(128)} %stack.175.ids, bf16[1024,1024]{1,0:T(8,128)(2,1)} %get-tuple-element.104.nt_ref, bf16[1024,1024]{1,0:T(8,128)(2,1)} %get-tuple-element.107.d_ref.dy_ref, bf16[1024,1024]{1,0:T(8,128)(2,1)} %get-tuple-element.136.o_ref, ...), custom_call_target="tpu_custom_call" | custom-call | flops 19549999104 | bytes 1024 | tf_op jit(solution)/shard_map/pallas_call | solution.py:435
  143.1 4.1 slice_bitcast_fusion.5
  157.7 40.2 %shard_map.173 = (bf16[2,512,2048]{2,1,0:T(8,128)(2,1)}, bf16[2,512,2048]{2,1,0:T(8,128)(2,1)}, f32[1,2048]{1,0:T(1,128)}, f32[1024,1024]{1,0:T(8,128)}, f32[1024,1024]{1,0:T(8,128)}) custom-call(s32[9]{0:T(128)} %stack.174.ids, bf16[1024,1024]{1,0:T(8,128)(2,1)} %get-tuple-element.127.n_ref, bf16[1024,1024]{1,0:T(8,128)(2,1)} %get-tuple-element.104.nt_ref, ...), custom_call_target="tpu_custom_call" | custom-call | flops 49450000384 | bytes 1024 | tf_op jit(solution)/shard_map/pallas_call | solution.py:204
  197.9 4.2 slice_bitcast_fusion
  210.1 3.1 add_convert_fusion.7
  213.9 25.2 %shard_map.174 = (bf16[2,512,1024]{2,1,0:T(8,128)(2,1)}, bf16[2,512,1024]{2,1,0:T(8,128)(2,1)}, f32[1,1024]{1,0:T(1,128)}, f32[1024,1024]{1,0:T(8,128)}, f32[1024,1024]{1,0:T(8,128)}) custom-call(s32[9]{0:T(128)} %stack.174.ids, bf16[1024,1024]{1,0:T(8,128)(2,1)} %get-tuple-element.127.n_ref, bf16[1024,1024]{1,0:T(8,128)(2,1)} %get-tuple-element.104.nt_ref, ...), custom_call_target="tpu_custom_call" | custom-call | flops 24725000192 | bytes 1024 | tf_op jit(solution)/shard_map/pallas_call | solution.py:204
  248.8 8.5 %collective-permute-done.27 = bf16[2,256,2048]{2,1,0:T(8,128)(2,1)} collective-permute-done((bf16[2,256,2048]{2,1,0:T(8,128)(2,1)}, bf16[2,256,2048]{2,1,0:T(8,128)(2,1)}, u32[]{:S(2)}, u32[]{:S(2)}) %collective-permute-start.27) | collective-permute-done | bytes 2097184 | tf_op jit(solution)/shard_map/ppermute | solution.py:709
  257.4 22.5 %collective-permute-done.21 = bf16[2,128,2048]{2,1,0:T(8,128)(2,1)} collective-permute-done((bf16[2,128,2048]{2,1,0:T(8,128)(2,1)}, bf16[2,128,2048]{2,1,0:T(8,128)(2,1)}, u32[]{:S(2)}, u32[]{:S(2)}) %collective-permute-start.21) | collective-permute-done | bytes 1048608 | tf_op jit(solution)/shard_map/ppermute | solution.py:713
  283.4 3.8 add_convert_fusion.5
  287.3 25.2 %shard_map.175 = (bf16[2,512,1024]{2,1,0:T(8,128)(2,1)}, bf16[2,512,1024]{2,1,0:T(8,128)(2,1)}, f32[1,1024]{1,0:T(1,128)}, f32[1024,1024]{1,0:T(8,128)}, f32[1024,1024]{1,0:T(8,128)}) custom-call(s32[9]{0:T(128)} %stack.174.ids, bf16[1024,1024]{1,0:T(8,128)(2,1)} %get-tuple-element.127.n_ref, bf16[1024,1024]{1,0:T(8,128)(2,1)} %get-tuple-element.104.nt_ref, ...), custom_call_target="tpu_custom_call" | custom-call | flops 24725000192 | bytes 1024 | tf_op jit(solution)/shard_map/pallas_call | solution.py:204
  320.8 3.1 add_convert_fusion.2
  323.9 6.1 %collective-permute-done.24 = bf16[128,2048]{1,0:T(8,128)(2,1)} collective-permute-done((bf16[128,2048]{1,0:T(8,128)(2,1)}, bf16[128,2048]{1,0:T(8,128)(2,1)}, u32[]{:S(2)}, u32[]{:S(2)}) %collective-permute-start.24) | collective-permute-done | bytes 524320 | tf_op jit(solution)/shard_map/ppermute | solution.py:719
  331.9 3.7 collective-permute-start.41
  339.2 3.3 collective-permute-done.28
  347.2 20.0 %shard_map.176 = (bf16[1024,1024]{1,0:T(8,128)(2,1)}, bf16[1024,1024]{1,0:T(8,128)(2,1)}, f32[8,1024]{1,0:T(8,128)}) custom-call(s32[10]{0:T(128)} %stack.170.ids, bf16[1024,1024]{1,0:T(8,128)(2,1)} %x_ref.3, bf16[1024,1024]{1,0:T(8,128)(2,1)} %get-tuple-element.107.d_ref.dy_ref, f32[1,1024]{1,0:T(1,128)} %bitcast.130, f32[1,1024]{1,0:T(1,128)} %bitcast.128, ...), custom_call_target="tpu_custom_call" | custom-call | flops 23000000512 | bytes 1024 | tf_op jit(solution)/shard_map/pallas_call | solution.py:501
  375.6 15.6 %collective-permute-done.48 = bf16[128,1024]{1,0:T(8,128)(2,1)S(1)} collective-permute-done((bf16[128,1024]{1,0:T(8,128)(2,1)S(1)}, bf16[128,1024]{1,0:T(8,128)(2,1)S(1)}, u32[]{:S(2)}, u32[]{:S(2)}) %collective-permute-start.48) | collective-permute-done | bytes 262176 | tf_op jit(solution)/shard_map/ppermute | solution.py:719
  395.3 3.7 collective-permute-start.46
  399.1 6.4 %collective-permute-done.42.rm = bf16[128,2048]{1,0:T(8,128)(2,1)S(1)} collective-permute-done((bf16[128,2048]{1,0:T(8,128)(2,1)S(1)}, bf16[128,2048]{1,0:T(8,128)(2,1)S(1)}, u32[]{:S(2)}, u32[]{:S(2)}) %collective-permute-start.42) | collective-permute-done | bytes 524320 | tf_op jit(solution)/shard_map/ppermute | solution.py:725
  405.6 16.5 %collective-permute-start.54 = (bf16[128,1024]{1,0:T(8,128)(2,1)S(1)}, bf16[128,1024]{1,0:T(8,128)(2,1)S(1)}, u32[]{:S(2)}, u32[]{:S(2)}) collective-permute-start(bf16[128,1024]{1,0:T(8,128)(2,1)S(1)} %fusion.6), channel_id=1, source_target_pairs={{0,24},{4,28},{8,16},{12,20},{16,8},{20,12},{24,0},{28,4},{1,25},{... | collective-permute-start | bytes 786440 | tf_op jit(solution)/shard_map/ppermute | solution.py:722
  423.5 5.2 %collective-permute-start.40 = (bf16[128,1024]{1,0:T(8,128)(2,1)S(1)}, bf16[128,1024]{1,0:T(8,128)(2,1)S(1)}, u32[]{:S(2)}, u32[]{:S(2)}) collective-permute-start(bf16[128,1024]{1,0:T(8,128)(2,1)S(1)} %select_bitcast_fusion.3), channel_id=1, source_target_pairs={{0,8},{4,12},{8,0},{12,4},{16,24},{20,28},{24,16},{28,20},{1,9},{5... | collective-permute-start | bytes 786440 | tf_op jit(solution)/shard_map/ppermute | solution.py:719
  430.5 11.8 %shard_map.177 = (f32[256,12288]{1,0:T(8,128)}, f32[256,12288]{1,0:T(8,128)}, f32[256,12288]{1,0:T(8,128)}, f32[256,12288]{1,0:T(8,128)}) custom-call(s32[2]{0:T(128)} %pad_add_fusion.ids, bf16[128,2048]{1,0:T(8,128)(2,1)} %copy-done.21, bf16[128,2048]{1,0:T(8,128)(2,1)} %copy-done.46, bf16[128,2048]{1,0:T(8,128)(2,1)} %copy-done.45, ...), custom_call_target="tpu_custom_call" | custom-call | flops 13799999488 | bytes 1024 | tf_op jit(solution)/shard_map/pallas_call | solution.py:572
  455.2 7.7 %collective-permute-done.64 = f32[56,128]{1,0:T(8,128)S(1)} collective-permute-done((f32[56,128]{1,0:T(8,128)S(1)}, f32[56,128]{1,0:T(8,128)S(1)}, u32[]{:S(2)}, u32[]{:S(2)}) %collective-permute-start.64) | collective-permute-done | bytes 28704 | tf_op jit(solution)/shard_map/ppermute | solution.py:791
  465.4 11.8 %shard_map.178 = (f32[256,12288]{1,0:T(8,128)}, f32[256,12288]{1,0:T(8,128)}, f32[256,12288]{1,0:T(8,128)}, f32[256,12288]{1,0:T(8,128)}) custom-call(s32[2]{0:T(128)} %pad_add_fusion.ids, bf16[128,2048]{1,0:T(8,128)(2,1)} %copy-done.7, bf16[128,2048]{1,0:T(8,128)(2,1)} %copy-done.18, ...), custom_call_target="tpu_custom_call", output_to_operand_aliasing={{0}: (8, {}), {1}: (9, {}), {2}: (10, {}), {3}: (11, {})} | custom-call | flops 13799999488 | bytes 1024 | tf_op jit(solution)/shard_map/pallas_call | solution.py:572
  478.1 6.9 %shard_map.179 = (f32[256,12288]{1,0:T(8,128)}, f32[256,12288]{1,0:T(8,128)}, f32[256,12288]{1,0:T(8,128)}, f32[256,12288]{1,0:T(8,128)}) custom-call(s32[2]{0:T(128)} %pad_add_fusion.ids, bf16[128,1024]{1,0:T(8,128)(2,1)} %copy-done.15, bf16[128,1024]{1,0:T(8,128)(2,1)} %copy-done.28, ...), custom_call_target="tpu_custom_call", output_to_operand_aliasing={{0}: (8, {}), {1}: (9, {}), {2}: (10, {}), {3}: (11, {})} | custom-call | flops 6899999744 | bytes 1024 | tf_op jit(solution)/shard_map/pallas_call | solution.py:572
  485.7 6.9 %shard_map.180 = (f32[256,12288]{1,0:T(8,128)}, f32[256,12288]{1,0:T(8,128)}, f32[256,12288]{1,0:T(8,128)}, f32[256,12288]{1,0:T(8,128)}) custom-call(s32[2]{0:T(128)} %pad_add_fusion.ids, bf16[128,1024]{1,0:T(8,128)(2,1)} %copy-done.14, bf16[128,1024]{1,0:T(8,128)(2,1)} %copy-done.27, ...), custom_call_target="tpu_custom_call", output_to_operand_aliasing={{0}: (8, {}), {1}: (9, {}), {2}: (10, {}), {3}: (11, {})} | custom-call | flops 6899999744 | bytes 1024 | tf_op jit(solution)/shard_map/pallas_call | solution.py:572
  (262 shorter events, 108.2 us)
Async XLA Ops:
  2.0 26.2 %collective-permute-start.1 = (bf16[128,4096]{1,0:T(8,128)(2,1)S(1)}, bf16[128,4096]{1,0:T(8,128)(2,1)S(1)}, u32[]{:S(2)}, u32[]{:S(2)}) collective-permute-start(bf16[128,4096]{1,0:T(8,128)(2,1)S(1)} %constant_dynamic-slice_fusion), channel_id=1, source_target_pairs={{0,2},{1,3},{2,0},{3,1},{4,6},{5,7},{6,4},{7,5},{8,10},{9,11},{10,... | collective-permute-start | bytes 3145736 | tf_op jit(solution)/shard_map/ppermute | solution.py:640
  5.0 24.7 %collective-permute-start = (bf16[128,4096]{1,0:T(8,128)(2,1)S(1)}, bf16[128,4096]{1,0:T(8,128)(2,1)}, u32[]{:S(2)}, u32[]{:S(2)}) collective-permute-start(bf16[128,4096]{1,0:T(8,128)(2,1)S(1)} %constant_dynamic-slice_fusion), channel_id=1, source_target_pairs={{0,1},{1,0},{2,3},{3,2},{4,5},{5,4},{6,7},{7,6},{8,9},{9,8},{10,11... | collective-permute-start | bytes 3145736 | tf_op jit(solution)/shard_map/ppermute | solution.py:640
  48.8 48.0 %collective-permute-start.5 = (bf16[128,8192]{1,0:T(8,128)(2,1)S(1)}, bf16[128,8192]{1,0:T(8,128)(2,1)S(1)}, u32[]{:S(2)}, u32[]{:S(2)}) collective-permute-start(bf16[128,8192]{1,0:T(8,128)(2,1)S(1)} %dynamic-slice), channel_id=1, source_target_pairs={{0,2},{1,3},{2,0},{3,1},{4,6},{5,7},{6,4},{7,5},{8,10},{9,11},{10,... | collective-permute-start | bytes 6291464 | tf_op jit(solution)/shard_map/ppermute | solution.py:640
  49.4 47.9 %collective-permute-start.4 = (bf16[128,8192]{1,0:T(8,128)(2,1)S(1)}, bf16[128,8192]{1,0:T(8,128)(2,1)}, u32[]{:S(2)}, u32[]{:S(2)}) collective-permute-start(bf16[128,8192]{1,0:T(8,128)(2,1)S(1)} %dynamic-slice), channel_id=1, source_target_pairs={{0,1},{1,0},{2,3},{3,2},{4,5},{5,4},{6,7},{7,6},{8,9},{9,8},{10,11... | collective-permute-start | bytes 6291464 | tf_op jit(solution)/shard_map/ppermute | solution.py:640
  99.6 26.5 %collective-permute-start.12 = (bf16[128,8192]{1,0:T(8,128)(2,1)}, bf16[128,8192]{1,0:T(8,128)(2,1)}, u32[]{:S(2)}, u32[]{:S(2)}) collective-permute-start(bf16[128,8192]{1,0:T(8,128)(2,1)} %collective-permute-done.4.refs_1_.refs_10_), channel_id=1, source_target_pairs={{0,4},{4,0},{8,12},{12,8},{16,20},{20,16},{24,28},{28,24},{1,5},{5... | collective-permute-start | bytes 6291464 | tf_op jit(solution)/shard_map/ppermute | solution.py:647
  100.1 26.0 %collective-permute-start.13 = (bf16[128,8192]{1,0:T(8,128)(2,1)S(1)}, bf16[128,8192]{1,0:T(8,128)(2,1)}, u32[]{:S(2)}, u32[]{:S(2)}) collective-permute-start(bf16[128,8192]{1,0:T(8,128)(2,1)S(1)} %copy-done.23), channel_id=1, source_target_pairs={{0,4},{4,0},{8,12},{12,8},{16,20},{20,16},{24,28},{28,24},{1,5},{5... | collective-permute-start | bytes 6291464 | tf_op jit(solution)/shard_map/ppermute | solution.py:647
  100.3 25.5 %collective-permute-start.11 = (bf16[64,8192]{1,0:T(8,128)(2,1)S(1)}, bf16[64,8192]{1,0:T(8,128)(2,1)S(1)}, u32[]{:S(2)}, u32[]{:S(2)}) collective-permute-start(bf16[64,8192]{1,0:T(8,128)(2,1)S(1)} %slice.212), channel_id=1, source_target_pairs={{0,1},{1,0},{2,3},{3,2},{4,5},{5,4},{6,7},{7,6},{8,9},{9,8},{10,11... | collective-permute-start | bytes 3145736 | tf_op jit(solution)/shard_map/ppermute | solution.py:644
  100.9 25.3 %collective-permute-start.10 = (bf16[64,8192]{1,0:T(8,128)(2,1)S(1)}, bf16[64,8192]{1,0:T(8,128)(2,1)}, u32[]{:S(2)}, u32[]{:S(2)}) collective-permute-start(bf16[64,8192]{1,0:T(8,128)(2,1)S(1)} %slice.211), channel_id=1, source_target_pairs={{0,2},{1,3},{2,0},{3,1},{4,6},{5,7},{6,4},{7,5},{8,10},{9,11},{10,... | collective-permute-start | bytes 3145736 | tf_op jit(solution)/shard_map/ppermute | solution.py:644
  154.9 55.1 %collective-permute-start.18 = (bf16[2,256,2048]{2,1,0:T(8,128)(2,1)}, bf16[2,256,2048]{2,1,0:T(8,128)(2,1)}, u32[]{:S(2)}, u32[]{:S(2)}) collective-permute-start(bf16[2,256,2048]{2,1,0:T(8,128)(2,1)} %add_convert_fusion.1), channel_id=1, source_target_pairs={{0,2},{1,3},{2,0},{3,1},{4,6},{5,7},{6,4},{7,5},{8,10},{9,11},{10,... | collective-permute-start | bytes 6291464 | tf_op jit(solution)/shard_map/ppermute | solution.py:709
  208.6 48.8 %collective-permute-start.27 = (bf16[2,256,2048]{2,1,0:T(8,128)(2,1)}, bf16[2,256,2048]{2,1,0:T(8,128)(2,1)}, u32[]{:S(2)}, u32[]{:S(2)}) collective-permute-start(bf16[2,256,2048]{2,1,0:T(8,128)(2,1)} %add_convert_fusion), channel_id=1, source_target_pairs={{0,1},{1,0},{2,3},{3,2},{4,5},{5,4},{6,7},{7,6},{8,9},{9,8},{10,11... | collective-permute-start | bytes 6291464 | tf_op jit(solution)/shard_map/ppermute | solution.py:709
  213.2 66.6 %collective-permute-start.21 = (bf16[2,128,2048]{2,1,0:T(8,128)(2,1)}, bf16[2,128,2048]{2,1,0:T(8,128)(2,1)}, u32[]{:S(2)}, u32[]{:S(2)}) collective-permute-start(bf16[2,128,2048]{2,1,0:T(8,128)(2,1)} %add_convert_fusion.7), channel_id=1, source_target_pairs={{0,1},{1,0},{2,3},{3,2},{4,5},{5,4},{6,7},{7,6},{8,9},{9,8},{10,11... | collective-permute-start | bytes 3145736 | tf_op jit(solution)/shard_map/ppermute | solution.py:713
  242.3 41.1 %collective-permute-start.26 = (bf16[256,2048]{1,0:T(8,128)(2,1)}, bf16[256,2048]{1,0:T(8,128)(2,1)S(1)}, u32[]{:S(2)}, u32[]{:S(2)}) collective-permute-start(bf16[256,2048]{1,0:T(8,128)(2,1)} %get-tuple-element.176), channel_id=1, source_target_pairs={{0,4},{4,0},{8,12},{12,8},{16,20},{20,16},{24,28},{28,24},{1,5},{5... | collective-permute-start | bytes 3145736 | tf_op jit(solution)/shard_map/ppermute | solution.py:686
  244.7 38.7 %collective-permute-start.25 = (bf16[256,2048]{1,0:T(8,128)(2,1)}, bf16[256,2048]{1,0:T(8,128)(2,1)S(1)}, u32[]{:S(2)}, u32[]{:S(2)}) collective-permute-start(bf16[256,2048]{1,0:T(8,128)(2,1)} %get-tuple-element.177), channel_id=1, source_target_pairs={{0,4},{4,0},{8,12},{12,8},{16,20},{20,16},{24,28},{28,24},{1,5},{5... | collective-permute-start | bytes 3145736 | tf_op jit(solution)/shard_map/ppermute | solution.py:686
  247.5 82.5 %collective-permute-start.31 = (bf16[2,256,1024]{2,1,0:T(8,128)(2,1)}, bf16[2,256,1024]{2,1,0:T(8,128)(2,1)}, u32[]{:S(2)}, u32[]{:S(2)}) collective-permute-start(bf16[2,256,1024]{2,1,0:T(8,128)(2,1)} %add_convert_fusion.4), channel_id=1, source_target_pairs={{0,1},{1,0},{2,3},{3,2},{4,5},{5,4},{6,7},{7,6},{8,9},{9,8},{10,11... | collective-permute-start | bytes 3145736 | tf_op jit(solution)/shard_map/ppermute | solution.py:709
  317.4 25.1 %collective-permute-start.28 = (bf16[2,128,2048]{2,1,0:T(8,128)(2,1)}, bf16[2,128,2048]{2,1,0:T(8,128)(2,1)}, u32[]{:S(2)}, u32[]{:S(2)}) collective-permute-start(bf16[2,128,2048]{2,1,0:T(8,128)(2,1)} %add_convert_fusion.5), channel_id=1, source_target_pairs={{0,2},{1,3},{2,0},{3,1},{4,6},{5,7},{6,4},{7,5},{8,10},{9,11},{10,... | collective-permute-start | bytes 3145736 | tf_op jit(solution)/shard_map/ppermute | solution.py:713
  330.0 62.5 %collective-permute-start.36 = (bf16[256,1024]{1,0:T(8,128)(2,1)}, bf16[256,1024]{1,0:T(8,128)(2,1)}, u32[]{:S(2)}, u32[]{:S(2)}) collective-permute-start(bf16[256,1024]{1,0:T(8,128)(2,1)} %get-tuple-element.184), channel_id=1, source_target_pairs={{0,4},{4,0},{8,12},{12,8},{16,20},{20,16},{24,28},{28,24},{1,5},{5... | collective-permute-start | bytes 1572872 | tf_op jit(solution)/shard_map/ppermute | solution.py:686
  330.0 62.5 %collective-permute-start.37 = (bf16[256,1024]{1,0:T(8,128)(2,1)}, bf16[256,1024]{1,0:T(8,128)(2,1)}, u32[]{:S(2)}, u32[]{:S(2)}) collective-permute-start(bf16[256,1024]{1,0:T(8,128)(2,1)} %get-tuple-element.185), channel_id=1, source_target_pairs={{0,4},{4,0},{8,12},{12,8},{16,20},{20,16},{24,28},{28,24},{1,5},{5... | collective-permute-start | bytes 1572872 | tf_op jit(solution)/shard_map/ppermute | solution.py:686
  331.9 39.7 %collective-permute-start.41 = (bf16[128,2048]{1,0:T(8,128)(2,1)S(1)}, bf16[128,2048]{1,0:T(8,128)(2,1)}, u32[]{:S(2)}, u32[]{:S(2)}) collective-permute-start(bf16[128,2048]{1,0:T(8,128)(2,1)S(1)} %fusion.3), channel_id=1, source_target_pairs={{0,24},{4,28},{8,16},{12,20},{16,8},{20,12},{24,0},{28,4},{1,25},{... | collective-permute-start | bytes 1572872 | tf_op jit(solution)/shard_map/ppermute | solution.py:722
  335.6 56.0 %collective-permute-start.38 = (bf16[2,256,1024]{2,1,0:T(8,128)(2,1)}, bf16[2,256,1024]{2,1,0:T(8,128)(2,1)S(1)}, u32[]{:S(2)}, u32[]{:S(2)}) collective-permute-start(bf16[2,256,1024]{2,1,0:T(8,128)(2,1)} %add_convert_fusion.2), channel_id=1, source_target_pairs={{0,1},{1,0},{2,3},{3,2},{4,5},{5,4},{6,7},{7,6},{8,9},{9,8},{10,11... | collective-permute-start | bytes 3145736 | tf_op jit(solution)/shard_map/ppermute | solution.py:709
  342.5 25.6 %collective-permute-start.47 = (bf16[2,128,1024]{2,1,0:T(8,128)(2,1)}, bf16[2,128,1024]{2,1,0:T(8,128)(2,1)}, u32[]{:S(2)}, u32[]{:S(2)}) collective-permute-start(bf16[2,128,1024]{2,1,0:T(8,128)(2,1)} %add_convert_fusion.13), channel_id=1, source_target_pairs={{0,2},{1,3},{2,0},{3,1},{4,6},{5,7},{6,4},{7,5},{8,10},{9,11},{10,... | collective-permute-start | bytes 1572872 | tf_op jit(solution)/shard_map/ppermute | solution.py:713
  371.6 19.6 %collective-permute-start.45 = (bf16[128,2048]{1,0:T(8,128)(2,1)S(1)}, bf16[128,2048]{1,0:T(8,128)(2,1)S(1)}, u32[]{:S(2)}, u32[]{:S(2)}) collective-permute-start(bf16[128,2048]{1,0:T(8,128)(2,1)S(1)} %copy-done.24), channel_id=1, source_target_pairs={{0,8},{4,12},{8,0},{12,4},{16,24},{20,28},{24,16},{28,20},{1,9},{5... | collective-permute-start | bytes 1572872 | tf_op jit(solution)/shard_map/ppermute | solution.py:719
  391.2 37.6 %collective-permute-start.43 = (bf16[128,2048]{1,0:T(8,128)(2,1)S(1)}, bf16[128,2048]{1,0:T(8,128)(2,1)S(1)}, u32[]{:S(2)}, u32[]{:S(2)}) collective-permute-start(bf16[128,2048]{1,0:T(8,128)(2,1)S(1)} %add_convert_fusion.10.sm), channel_id=1, source_target_pairs={{0,4},{4,0},{8,12},{12,8},{16,20},{20,16},{24,28},{28,24},{1,5},{5... | collective-permute-start | bytes 1572872 | tf_op jit(solution)/shard_map/ppermute | solution.py:732
  391.7 52.2 %collective-permute-start.62 = (f32[56,128]{1,0:T(8,128)S(1)}, f32[56,128]{1,0:T(8,128)S(1)}, u32[]{:S(2)}, u32[]{:S(2)}) collective-permute-start(f32[56,128]{1,0:T(8,128)S(1)} %fusion.14), channel_id=1, source_target_pairs={{0,2},{1,3},{2,0},{3,1},{4,6},{5,7},{6,4},{7,5},{8,10},{9,11},{10,... | collective-permute-start | bytes 86024 | tf_op jit(solution)/shard_map/ppermute | solution.py:789
  393.8 28.3 %collective-permute-start.39 = (bf16[2,128,1024]{2,1,0:T(8,128)(2,1)S(1)}, bf16[2,128,1024]{2,1,0:T(8,128)(2,1)S(1)}, u32[]{:S(2)}, u32[]{:S(2)}) collective-permute-start(bf16[2,128,1024]{2,1,0:T(8,128)(2,1)S(1)} %add_convert_fusion.12), channel_id=1, source_target_pairs={{0,2},{1,3},{2,0},{3,1},{4,6},{5,7},{6,4},{7,5},{8,10},{9,11},{10,... | collective-permute-start | bytes 1572872 | tf_op jit(solution)/shard_map/ppermute | solution.py:713
  395.3 28.2 %collective-permute-start.46 = (bf16[128,2048]{1,0:T(8,128)(2,1)S(1)}, bf16[128,2048]{1,0:T(8,128)(2,1)S(1)}, u32[]{:S(2)}, u32[]{:S(2)}) collective-permute-start(bf16[128,2048]{1,0:T(8,128)(2,1)S(1)} %fusion.2), channel_id=1, source_target_pairs={{0,24},{4,28},{8,16},{12,20},{16,8},{20,12},{24,0},{28,4},{1,25},{... | collective-permute-start | bytes 1572872 | tf_op jit(solution)/shard_map/ppermute | solution.py:722
  405.6 38.7 %collective-permute-start.54 = (bf16[128,1024]{1,0:T(8,128)(2,1)S(1)}, bf16[128,1024]{1,0:T(8,128)(2,1)S(1)}, u32[]{:S(2)}, u32[]{:S(2)}) collective-permute-start(bf16[128,1024]{1,0:T(8,128)(2,1)S(1)} %fusion.6), channel_id=1, source_target_pairs={{0,24},{4,28},{8,16},{12,20},{16,8},{20,12},{24,0},{28,4},{1,25},{... | collective-permute-start | bytes 786440 | tf_op jit(solution)/shard_map/ppermute | solution.py:722
  423.5 18.8 %collective-permute-start.40 = (bf16[128,1024]{1,0:T(8,128)(2,1)S(1)}, bf16[128,1024]{1,0:T(8,128)(2,1)S(1)}, u32[]{:S(2)}, u32[]{:S(2)}) collective-permute-start(bf16[128,1024]{1,0:T(8,128)(2,1)S(1)} %select_bitcast_fusion.3), channel_id=1, source_target_pairs={{0,8},{4,12},{8,0},{12,4},{16,24},{20,28},{24,16},{28,20},{1,9},{5... | collective-permute-start | bytes 786440 | tf_op jit(solution)/shard_map/ppermute | solution.py:719
  428.9 17.8 %collective-permute-start.53 = (bf16[128,2048]{1,0:T(8,128)(2,1)S(1)}, bf16[128,2048]{1,0:T(8,128)(2,1)S(1)}, u32[]{:S(2)}, u32[]{:S(2)}) collective-permute-start(bf16[128,2048]{1,0:T(8,128)(2,1)S(1)} %add_convert_fusion.8.sm), channel_id=1, source_target_pairs={{0,8},{4,12},{8,0},{12,4},{16,24},{20,28},{24,16},{28,20},{1,9},{5... | collective-permute-start | bytes 1572872 | tf_op jit(solution)/shard_map/ppermute | solution.py:725
  444.3 19.9 %collective-permute-start.58 = (bf16[128,2048]{1,0:T(8,128)(2,1)S(1)}, bf16[128,2048]{1,0:T(8,128)(2,1)S(1)}, u32[]{:S(2)}, u32[]{:S(2)}) collective-permute-start(bf16[128,2048]{1,0:T(8,128)(2,1)S(1)} %add_convert_fusion.8.sm), channel_id=1, source_target_pairs={{0,4},{4,0},{8,12},{12,8},{16,20},{20,16},{24,28},{28,24},{1,5},{5... | collective-permute-start | bytes 1572872 | tf_op jit(solution)/shard_map/ppermute | solution.py:732
  446.7 18.0 %collective-permute-start.59 = (bf16[128,2048]{1,0:T(8,128)(2,1)S(1)}, bf16[128,2048]{1,0:T(8,128)(2,1)S(1)}, u32[]{:S(2)}, u32[]{:S(2)}) collective-permute-start(bf16[128,2048]{1,0:T(8,128)(2,1)S(1)} %collective-permute-done.53.rm), channel_id=1, source_target_pairs={{0,4},{4,0},{8,12},{12,8},{16,20},{20,16},{24,28},{28,24},{1,5},{5... | collective-permute-start | bytes 1572872 | tf_op jit(solution)/shard_map/ppermute | solution.py:732
  464.1 20.9 %collective-permute-start.51 = (bf16[128,1024]{1,0:T(8,128)(2,1)S(1)}, bf16[128,1024]{1,0:T(8,128)(2,1)S(1)}, u32[]{:S(2)}, u32[]{:S(2)}) collective-permute-start(bf16[128,1024]{1,0:T(8,128)(2,1)S(1)} %add_convert_fusion.15.sm), channel_id=1, source_target_pairs={{0,4},{4,0},{8,12},{12,8},{16,20},{20,16},{24,28},{28,24},{1,5},{5... | collective-permute-start | bytes 786440 | tf_op jit(solution)/shard_map/ppermute | solution.py:732
  464.2 20.8 %collective-permute-start.52 = (bf16[128,1024]{1,0:T(8,128)(2,1)S(1)}, bf16[128,1024]{1,0:T(8,128)(2,1)S(1)}, u32[]{:S(2)}, u32[]{:S(2)}) collective-permute-start(bf16[128,1024]{1,0:T(8,128)(2,1)S(1)} %collective-permute-done.50.rm), channel_id=1, source_target_pairs={{0,4},{4,0},{8,12},{12,8},{16,20},{20,16},{24,28},{28,24},{1,5},{5... | collective-permute-start | bytes 786440 | tf_op jit(solution)/shard_map/ppermute | solution.py:732
  (81 other events, 841.6 us)
